TPU v7x, 512 devices: a whole 4x8x8 slice. The times are simulated.
512 devices in a mesh: fibre: 64 (over x, z, core), tm: 8 (over y).
Axes of the slice: x: 4, y: 8, z: 8, core: 2. Of those that a mesh axis runs over, the one named last changes fastest.
Arguments:
- recordings: float32 [8, 64, 6000, 128], P('tm', 'fibre'), may hold values from -100 to 100
- pair_blocks: int32 [64, 4, 2], P('fibre'), may hold values from 0 to 63, as said below
- pair_count: int32 [64], P('fibre'), may hold values from 1 to 4, as said below
Outputs:
- stacks: float32 [64, 8, 401, 128], P('fibre', 'tm')
Inputs may be any that keep to these rules, and one draw needn't show every extreme that they name: `pair_blocks`: every entry of owner o's list, live or not, lies in o .. min(o + 4, 63). `pair_count`: some owner has 4 live pairs in every draw.
All inputs are finite; a program needn't handle non-finite values.
Results may differ from a plain program's by a relative error of at most 0.0037.
Values may be sent and summed in bfloat16 or wider, within the bound.
No kernel may reach another device: no remote copies, remote signals or barrier semaphores. Data moves between devices by JAX's collectives and lax.ppermute only.
A program may use at most 64 MiB of HBM per device.

v0:
```python
import math

import jax
import jax.numpy as jnp
from jax import lax
from jax.sharding import PartitionSpec as P

FA = 48
FB = 125
TS = 6000
F0 = 60
NF = 1152
MAXLAG = 200
LAGS = 401
VS = 2
REACH = 4
MAXP = 4


EPSILON = 1e-06


def shifted(shard, axis, by):
    size = lax.axis_size(axis)
    pairs = [(i, i + by) for i in range(size) if 0 <= i + by < size]
    return lax.ppermute(shard, axis, pairs)


def whiten(real_part, imag_part):
    power = jnp.mean(real_part * real_part + imag_part * imag_part, axis=-2, keepdims=True)
    factor = lax.rsqrt(power + EPSILON)
    return jnp.concatenate([real_part * factor, imag_part * factor], axis=-2).astype(jnp.bfloat16)


def lag_table():
    lag_values = jnp.arange(LAGS, dtype=jnp.int32) - MAXLAG
    bin_values = jnp.arange(NF, dtype=jnp.int32) + F0
    phase = jnp.mod(lag_values[:, None] * bin_values[None, :], TS).astype(jnp.float32) * (
        2.0 * math.pi / TS
    )
    return jnp.concatenate([jnp.cos(phase), -jnp.sin(phase)], axis=1)


def cross_spectrum(source, receiver):
    src_values = source.astype(jnp.float32)
    rcv_values = receiver.astype(jnp.float32)
    src_real = src_values[:, :NF, :, None]
    src_imag = src_values[:, NF:, :, None]
    rcv_real = rcv_values[:, :NF, None, :]
    rcv_imag = rcv_values[:, NF:, None, :]
    real_part = jnp.sum(src_real * rcv_real + src_imag * rcv_imag, axis=0)
    imag_part = jnp.sum(src_real * rcv_imag - src_imag * rcv_real, axis=0)
    return jnp.concatenate([real_part, imag_part], axis=0)


def dft_band(samples):
    window_total = samples.shape[0]
    channels = samples.shape[2]
    highest = lax.Precision.HIGHEST
    split_samples = samples.reshape(window_total, FA, FB, channels)
    outer_index = jnp.arange(FA, dtype=jnp.int32)
    inner_index = jnp.arange(FB, dtype=jnp.int32)
    outer_phase = jnp.mod(outer_index[:, None] * outer_index[None, :], FA).astype(jnp.float32) * (
        2.0 * math.pi / FA
    )
    section_real = jnp.einsum(
        "kp,wpqc->wkqc", jnp.cos(outer_phase), split_samples, precision=highest
    )
    section_imag = -jnp.einsum(
        "kp,wpqc->wkqc", jnp.sin(outer_phase), split_samples, precision=highest
    )
    twist_phase = jnp.mod(outer_index[:, None] * inner_index[None, :], TS).astype(jnp.float32) * (
        2.0 * math.pi / TS
    )
    twist_cos = jnp.cos(twist_phase)[None, :, :, None]
    twist_sin = jnp.sin(twist_phase)[None, :, :, None]
    turned_real = section_real * twist_cos + section_imag * twist_sin
    turned_imag = section_imag * twist_cos - section_real * twist_sin
    inner_phase = jnp.mod(inner_index[:, None] * inner_index[None, :], FB).astype(jnp.float32) * (
        2.0 * math.pi / FB
    )
    inner_cos = jnp.cos(inner_phase)
    inner_sin = jnp.sin(inner_phase)
    final_real = jnp.einsum(
        "jq,wkqc->wjkc", inner_cos, turned_real, precision=highest
    ) + jnp.einsum("jq,wkqc->wjkc", inner_sin, turned_imag, precision=highest)
    final_imag = jnp.einsum(
        "jq,wkqc->wjkc", inner_cos, turned_imag, precision=highest
    ) - jnp.einsum("jq,wkqc->wjkc", inner_sin, turned_real, precision=highest)
    final_real = final_real.reshape(window_total, FB * FA, channels)[:, F0 : F0 + NF, :]
    final_imag = final_imag.reshape(window_total, FB * FA, channels)[:, F0 : F0 + NF, :]
    return (final_real, final_imag)


def shards(recordings, pair_blocks, pair_count):
    windows_here = recordings.shape[0]
    spectrum_real, spectrum_imag = dft_band(recordings[:, 0])
    whitened = whiten(spectrum_real, spectrum_imag)
    channels = whitened.shape[2]
    pieces = [whitened]
    for distance in range(1, REACH + 1):
        pieces.append(shifted(whitened, "fibre", -distance))
    stacked = jnp.stack(pieces, axis=0)
    sources = stacked[:, :, :, :: channels // VS]
    owner_index = lax.axis_index("fibre")
    lag_weights = lag_table()
    pair_list = pair_blocks[0]
    pair_total = pair_count[0]
    initial = jnp.zeros((MAXP, VS, LAGS, channels), jnp.float32)

    def one_pair(slot_index, totals):
        source_offset = pair_list[slot_index, 0] - owner_index
        receiver_offset = pair_list[slot_index, 1] - owner_index
        source = lax.dynamic_index_in_dim(sources, source_offset, 0, keepdims=False)
        receiver = lax.dynamic_index_in_dim(stacked, receiver_offset, 0, keepdims=False)
        spectrum = cross_spectrum(source, receiver)
        result = jnp.einsum("lf,fjc->jlc", lag_weights, spectrum, precision=lax.Precision.HIGHEST)
        return lax.dynamic_update_index_in_dim(totals, result, slot_index, 0)

    totals = lax.fori_loop(0, pair_total, one_pair, initial)
    partial_stack = totals.reshape(MAXP * VS, LAGS, channels)
    summed = lax.psum_scatter(partial_stack, "tm", scatter_dimension=0, tiled=True)
    stack_scale = 1.0 / math.sqrt(NF * windows_here * lax.axis_size("tm"))
    return (summed * stack_scale)[None]


def solution(mesh):
    in_specs = (P("tm", "fibre", None, None), P("fibre", None, None), P("fibre"))
    out_specs = P("fibre", "tm", None, None)
    return jax.shard_map(shards, mesh=mesh, in_specs=in_specs, out_specs=out_specs, check_vma=False)
```

profile of v0, /device:TPU:2, one launch (start us, length us, event | category | flops | bytes accessed | tf_op | source)
XLA Modules:
  0.0 243.6 jit_solution(12718230890422391191)
XLA Ops:
  6.8 2.0 reshape.199
  8.8 4.5 %fusion.28 = f32[48,125,128]{2,0,1:T(8,128)S(1)} fusion(f32[48,125,128]{2,1,0:T(8,128)S(1)} %reshape.199), kind=kOutput, calls=%fused_computation.37 | convolution fusion | flops 442388736 | bytes 6144000 | tf_op jit(solution)/shard_map/kp,wpqc->wkqc/dot_general | solution.py:69
  13.3 5.9 %fusion.17 = (f32[48,125,128]{2,0,1:T(8,128)S(1)}, f32[48,125,128]{2,0,1:T(8,128)S(1)}) fusion(f32[48,125,128]{2,0,1:T(8,128)S(1)} %fusion.28, f32[48,125]{0,1:T(8,128)S(1)} %get-tuple-element.103, f32[48,125]{0,1:T(8,128)S(1)} %get-tuple-element.104, f32[48,125,128]{2,1,0:T(8,128)S(1)} %reshape.199), kind=kOutput, calls=%fused_computation.24 | convolution fusion | flops 447764736 | bytes 12336000 | tf_op jit(solution)/shard_map/kp,wpqc->wkqc/dot_general | solution.py:66
  19.2 4.4 %fusion.20 = f32[48,128,125]{1,2,0:T(8,128)S(1)} fusion(f32[48,125,128]{2,0,1:T(8,128)S(1)} %get-tuple-element.98), kind=kOutput, calls=%fused_computation.29 | convolution fusion | flops 1152140672 | bytes 6144000 | tf_op jit(solution)/shard_map/jq,wkqc->wjkc/dot_general | solution.py:87
  23.6 4.1 %fusion.22 = f32[48,128,125]{1,2,0:T(8,128)S(1)} fusion(f32[48,125,128]{2,0,1:T(8,128)S(1)} %get-tuple-element.98), kind=kOutput, calls=%fused_computation.31 | convolution fusion | flops 1152140672 | bytes 6144000 | tf_op jit(solution)/shard_map/jq,wkqc->wjkc/dot_general | solution.py:86
  27.7 4.2 %subtract_bitcast_fusion = f32[1,125,48,128]{3,1,2,0:T(8,128)S(1)} fusion(f32[48,128,125]{1,2,0:T(8,128)S(1)} %fusion.20, f32[48,125,128]{2,0,1:T(8,128)S(1)} %get-tuple-element.97), kind=kOutput, calls=%fused_computation.19 | convolution fusion | flops 1152908672 | bytes 9216000 | tf_op jit(solution)/shard_map/jq,wkqc->wjkc/dot_general | solution.py:89
  31.9 1.8 copy.29
  33.7 14.6 %add_bitcast_fusion = f32[1,125,48,128]{3,1,2,0:T(8,128)S(1)} fusion(f32[48,128,125]{1,2,0:T(8,128)S(1)} %fusion.22, f32[48,125,128]{2,0,1:T(8,128)S(1)} %get-tuple-element.97), kind=kOutput, calls=%fused_computation.20 | convolution fusion | flops 1152908672 | bytes 9216000 | tf_op jit(solution)/shard_map/jq,wkqc->wjkc/dot_general | solution.py:84
  48.3 1.8 copy.26
  50.5 10.4 %collective-permute-start = (bf16[1,2304,128]{2,1,0:T(8,128)(2,1)S(1)}, bf16[1,2304,128]{2,1,0:T(8,128)(2,1)}, u32[]{:S(2)}, u32[]{:S(2)}) collective-permute-start(bf16[1,2304,128]{2,1,0:T(8,128)(2,1)S(1)} %pad_maximum_fusion.1), channel_id=1, source_target_pairs={{8,0},{16,8},{24,16},{32,24},{40,32},{48,40},{56,48},{64,56},{72,6... | collective-permute-start | bytes 1769480 | tf_op jit(solution)/shard_map/ppermute | solution.py:26
  60.9 2.5 %collective-permute-start.1 = (bf16[1,2304,128]{2,1,0:T(8,128)(2,1)S(1)}, bf16[1,2304,128]{2,1,0:T(8,128)(2,1)}, u32[]{:S(2)}, u32[]{:S(2)}) collective-permute-start(bf16[1,2304,128]{2,1,0:T(8,128)(2,1)S(1)} %pad_maximum_fusion.1), channel_id=1, source_target_pairs={{16,0},{24,8},{32,16},{40,24},{48,32},{56,40},{64,48},{72,56},{80,... | collective-permute-start | bytes 1769480 | tf_op jit(solution)/shard_map/ppermute | solution.py:26
  63.4 2.3 collective-permute-start.2
  65.6 2.2 collective-permute-start.3
  67.9 8.9 %fusion.40 = (f32[401,1152]{1,0:T(8,128)}, f32[401,1152]{1,0:T(8,128)}) fusion(s32[1152]{0:T(1024)S(1)} %iota_add_fusion, s32[401]{0:T(512)S(1)} %iota_add_fusion.1), kind=kLoop, calls=%fused_computation.48 | loop fusion | flops 4619520 | bytes 3701828 | tf_op jit(solution)/shard_map/cos | solution.py:41
  76.8 4.1 %pad_maximum_fusion = f32[401,2304]{1,0:T(8,128)} fusion(f32[401,1152]{1,0:T(8,128)} %get-tuple-element.100, f32[401,1152]{1,0:T(8,128)} %get-tuple-element.99), kind=kLoop, calls=%fused_computation.18 | loop fusion | flops 923904 | bytes 7391232 | tf_op jit(solution)/shard_map/concatenate | solution.py:41
  82.1 9.8 %collective-permute-done.1 = bf16[1,2304,128]{2,1,0:T(8,128)(2,1)} collective-permute-done((bf16[1,2304,128]{2,1,0:T(8,128)(2,1)S(1)}, bf16[1,2304,128]{2,1,0:T(8,128)(2,1)}, u32[]{:S(2)}, u32[]{:S(2)}) %collective-permute-start.1) | collective-permute-done | bytes 589856 | tf_op jit(solution)/shard_map/ppermute | solution.py:26
  93.0 23.7 %collective-permute-done.2 = bf16[1,2304,128]{2,1,0:T(8,128)(2,1)} collective-permute-done((bf16[1,2304,128]{2,1,0:T(8,128)(2,1)S(1)}, bf16[1,2304,128]{2,1,0:T(8,128)(2,1)}, u32[]{:S(2)}, u32[]{:S(2)}) %collective-permute-start.2) | collective-permute-done | bytes 589856 | tf_op jit(solution)/shard_map/ppermute | solution.py:26
  117.9 7.3 %collective-permute-done.3 = bf16[1,2304,128]{2,1,0:T(8,128)(2,1)} collective-permute-done((bf16[1,2304,128]{2,1,0:T(8,128)(2,1)S(1)}, bf16[1,2304,128]{2,1,0:T(8,128)(2,1)}, u32[]{:S(2)}, u32[]{:S(2)}) %collective-permute-start.3) | collective-permute-done | bytes 589856 | tf_op jit(solution)/shard_map/ppermute | solution.py:26
  126.3 20.7 %slice.23 = bf16[5,1,2304,2]{3,2,1,0:T(8,128)(2,1)} slice(bf16[5,1,2304,128]{3,2,1,0:T(8,128)(2,1)S(1)} %bitcast_dynamic-update-slice_fusion), slice={[0:5:1], [0:1:1], [0:2304:1], [0:128:64]} | slice | bytes 92160 | tf_op jit(solution)/shard_map/slice | solution.py:104
  147.0 2.5 %copy.30 = bf16[5,1,2304,2]{2,3,1,0:T(2,128)(2,1)S(1)} copy(bf16[5,1,2304,2]{3,2,1,0:T(8,128)(2,1)} %slice.23) | data formatting | bytes 92160 | tf_op jit(solution)/shard_map/while | solution.py:120
  149.4 1.3 broadcast_in_dim.7
  150.7 10.7 %while.10 = (s32[]{:T(128)}, f32[4,2,401,128]{3,2,1,0:T(8,128)}, s32[]{:T(128)}, s32[4,2]{0,1:T(2,128)S(1)}, s32[]{:T(128)}, /*index=5*/bf16[5,1,2304,2]{2,3,1,0...) while((s32[]{:T(128)}, f32[4,2,401,128]{3,2,1,0:T(8,128)}, ...), condition=%wide.region_2.3_spmd, body=%wide.region_1.2_spmd.sunk | while | flops 2840891904 | bytes 37881160 | solution.py:120
  154.6 6.2 %fusion.120 = f32[4,2,401,128]{3,2,1,0:T(8,128)} fusion(f32[4,2,401,128]{3,2,1,0:T(8,128)} %get-tuple-element.184, s32[]{:T(128)S(6)} %select_n.121, f32[401,2304]{1,0:T(8,128)} %get-tuple-element.202, f32[1152,2,128]{2,0,1:T(8,128)S(1)} %get-tuple-element.169, f32[1152,2,128]{2,0,1:T(8,128)S(1)} %get-tuple-element.170), kind=kOutput, calls=%fused_computation.6.clone.1 | convolution fusion | flops 2838822912 | bytes 6537220 | tf_op jit(solution)/shard_map/while/body/lf,fjc->jlc/dot_general | solution.py:117
  161.5 73.3 %reduce-scatter.4.cloned.1.call-done = f32[1,401,128]{2,1,0:T(8,128)} async-done(((f32[8,401,128]{2,1,0:T(8,128)}), f32[1,401,128]{2,1,0:T(8,128)}) %reduce-scatter.4.cloned.1.call-update) | async-done | bytes 205328
  (29 shorter events, 9.0 us)
Async XLA Ops:
  6.5 228.2 %reduce-scatter.4.cloned.1.call-start = ((), (), s32[]{:S(2)}) async-start(), calls=%async_computation.1 | async-start | bytes 1880064
  50.5 30.5 %collective-permute-start = (bf16[1,2304,128]{2,1,0:T(8,128)(2,1)S(1)}, bf16[1,2304,128]{2,1,0:T(8,128)(2,1)}, u32[]{:S(2)}, u32[]{:S(2)}) collective-permute-start(bf16[1,2304,128]{2,1,0:T(8,128)(2,1)S(1)} %pad_maximum_fusion.1), channel_id=1, source_target_pairs={{8,0},{16,8},{24,16},{32,24},{40,32},{48,40},{56,48},{64,56},{72,6... | collective-permute-start | bytes 1769480 | tf_op jit(solution)/shard_map/ppermute | solution.py:26
  60.9 31.0 %collective-permute-start.1 = (bf16[1,2304,128]{2,1,0:T(8,128)(2,1)S(1)}, bf16[1,2304,128]{2,1,0:T(8,128)(2,1)}, u32[]{:S(2)}, u32[]{:S(2)}) collective-permute-start(bf16[1,2304,128]{2,1,0:T(8,128)(2,1)S(1)} %pad_maximum_fusion.1), channel_id=1, source_target_pairs={{16,0},{24,8},{32,16},{40,24},{48,32},{56,40},{64,48},{72,56},{80,... | collective-permute-start | bytes 1769480 | tf_op jit(solution)/shard_map/ppermute | solution.py:26
  63.4 53.4 %collective-permute-start.2 = (bf16[1,2304,128]{2,1,0:T(8,128)(2,1)S(1)}, bf16[1,2304,128]{2,1,0:T(8,128)(2,1)}, u32[]{:S(2)}, u32[]{:S(2)}) collective-permute-start(bf16[1,2304,128]{2,1,0:T(8,128)(2,1)S(1)} %pad_maximum_fusion.1), channel_id=1, source_target_pairs={{24,0},{32,8},{40,16},{48,24},{56,32},{64,40},{72,48},{80,56},{88,... | collective-permute-start | bytes 1769480 | tf_op jit(solution)/shard_map/ppermute | solution.py:26
  65.6 59.5 %collective-permute-start.3 = (bf16[1,2304,128]{2,1,0:T(8,128)(2,1)S(1)}, bf16[1,2304,128]{2,1,0:T(8,128)(2,1)}, u32[]{:S(2)}, u32[]{:S(2)}) collective-permute-start(bf16[1,2304,128]{2,1,0:T(8,128)(2,1)S(1)} %pad_maximum_fusion.1), channel_id=1, source_target_pairs={{32,0},{40,8},{48,16},{56,24},{64,32},{72,40},{80,48},{88,56},{96,... | collective-permute-start | bytes 1769480 | tf_op jit(solution)/shard_map/ppermute | solution.py:26
  147.0 3.8 %copy-start.2 = (s32[1,4,2]{1,2,0:T(2,128)S(1)}, s32[1,4,2]{1,2,0:T(2,128)}, u32[]{:S(2)}) copy-start(s32[1,4,2]{1,2,0:T(2,128)} %param.6) | copy-start | bytes 100
  151.4 1.6 copy-start
  154.6 6.3 %copy-start.1 = (bf16[5,1,2304,128]{3,2,1,0:T(8,128)(2,1)S(1)}, bf16[5,1,2304,128]{3,2,1,0:T(8,128)(2,1)}, u32[]{:S(2)}) copy-start(bf16[5,1,2304,128]{3,2,1,0:T(8,128)(2,1)} %copy-done) | copy-start | bytes 8847364 | tf_op jit(solution)/shard_map/while
Sparse Core Ops, SparseCore 0:
  161.6 73.0 reduce-scatter.3
where the time goes:
time: 248 us; the launch traced here: 244 us
  waiting for transfers between devices  114 us (46%)
  matrix products  43.9 us (18%)
  local copies, waits for them, and re-layouts  36.6 us (15%)
  starting transfers between devices  17.3 us (7%)
  other arithmetic  15.5 us (6%)
  between operations  13.8 us (6%)
  loops' own time  2.57 us (1%)
    unnamed x2, waiting for transfers between devices  73.3 us
    ppermute x4, waiting for transfers between devices, shifted(): return lax.ppermute(shard, axis, pairs)  40.7 us
    slice x1, local copies, waits for them, and re-layouts, shards(): sources = stacked[:, :, :, ::channels // VS]  20.7 us
    ppermute x4, starting transfers between devices, shifted(): return lax.ppermute(shard, axis, pairs)  17.3 us
    dot_general x1, matrix products, dft_band(): jnp.einsum('jq,wkqc->wjkc', inner_cos, turned_real, precision=highest)  14.6 us
    cos x1, other arithmetic, lag_table(): return jnp.concatenate([jnp.cos(phase), -jnp.sin(phase)], axis=1)  8.92 us
    dot_general x1, matrix products, one_pair(): jnp.einsum('lf,fjc->jlc', lag_weights, spectrum, precision=lax.Precision....  6.24 us
    dot_general x1, matrix products, dft_band(): jnp.einsum('kp,wpqc->wkqc', jnp.cos(outer_phase), split_samples, precisio...  5.88 us
  transfers between devices with their start and end apart: 5, of which 4 were waited for; matrix products, arithmetic and copies ran while one was open for 7% of the time, Pallas kernels for 0%

commit v1 on v0

v1 whole, which is shorter than its diff:
```python
import functools
import math

import jax
import jax.numpy as jnp
import numpy as np
from jax import lax
from jax.experimental import pallas as pl
from jax.experimental.pallas import tpu as pltpu
from jax.sharding import PartitionSpec as P

TS = 6000
F0 = 60
NF = 1152
MAXLAG = 200
LAGS = 401
VS = 2
REACH = 4
MAXP = 4
EPSILON = 1e-06

QN = 75
PN = 80
KN = 38
KPAD = 40
QPAD = 80
SLOT = 32
GROUP = 2 * SLOT
FN = KN * GROUP
CHUNKS = FN // 128
SRC = 24
TAIL = 2 * SRC
ROWS = FN + TAIL
TABLE = FN + 2 * SRC - 1
HALF = 96
RANK = 2 * HALF
STEP = 16
BF = jnp.bfloat16
F32 = jnp.float32


def cos_table():
    index = np.arange(TS)
    folded = np.minimum(index, TS - index)
    sign = np.where(folded > TS // 4, -1.0, 1.0)
    folded = np.where(folded > TS // 4, TS // 2 - folded, folded)
    square = (folded * (2.0 * math.pi / TS)) ** 2
    value = np.ones(TS)
    for order in range(28, 0, -2):
        value = 1.0 - value * square / (order * (order - 1.0))
    return sign * value


COS = cos_table()


def cosine(index):
    return COS[np.mod(index, TS)]


def sine(index):
    return COS[np.mod(index - TS // 4, TS)]


def split(table):
    high = np.asarray(table, np.float32).astype(BF)
    low = (table - high.astype(np.float64)).astype(np.float32).astype(BF)
    return high, low


def bin_slots():
    bins = np.full((KN, SLOT), -1, np.int64)
    flipped = np.zeros((KN, SLOT), bool)
    for residue in range(KN):
        found = [(k, False) for k in range(F0, F0 + NF) if k % QN == residue]
        if residue:
            found += [(k, True) for k in range(F0, F0 + NF) if k % QN == QN - residue]
        for slot, (k, conj) in enumerate(found):
            bins[residue, slot] = k
            flipped[residue, slot] = conj
    return bins, flipped


def first_matrix():
    residue = np.arange(KN)[:, None]
    q = np.arange(QN)[None, :]
    weights = np.zeros((2 * KPAD, QPAD))
    weights[:KN, :QN] = cosine(PN * residue * q)
    weights[KPAD : KPAD + KN, :QN] = -sine(PN * residue * q)
    high, low = split(weights)
    zero = np.zeros_like(low)
    return np.concatenate(
        [np.concatenate([high, high], 1), np.concatenate([low, zero], 1)], 0
    )


def second_matrix():
    bins, flipped = bin_slots()
    p = np.arange(PN)
    weights = np.zeros((KN, GROUP, 2 * PN))
    cos = cosine(bins[:, :, None] * p)
    sin = sine(bins[:, :, None] * p)
    sign = np.where(flipped, -1.0, 1.0)[:, :, None]
    live = (bins >= 0).astype(np.float64)[:, :, None]
    weights[:, :SLOT, :PN] = live * cos
    weights[:, :SLOT, PN:] = live * sign * sin
    weights[:, SLOT:, :PN] = -live * sin
    weights[:, SLOT:, PN:] = live * sign * cos
    high, low = split(weights)
    return np.concatenate([high, low], 1)


def basis(table):
    rest = table.copy()
    columns = []
    for _ in range(HALF):
        norms = (rest * rest).sum(0)
        column = rest[:, int(norms.argmax())]
        for _ in range(2):
            for other in columns:
                column = column - other * np.cumsum(other * column)[-1]
        column = column / np.sqrt(np.cumsum(column * column)[-1])
        columns.append(column)
        rest = rest - column[:, None] * (column[:, None] * rest).sum(0)[None]
    return columns


@functools.lru_cache(None)
def lag_factors():
    bins, _ = bin_slots()
    live = (bins >= 0).astype(np.float64)
    lag = np.arange(MAXLAG + 1)[:, None]
    band = np.arange(F0, F0 + NF)[None, :]
    even_table = cosine(lag * band)
    odd_table = sine(lag[1:] * band)
    even = basis(even_table)
    odd = basis(odd_table)
    inner = np.zeros((RANK, KN, 2, SLOT))
    place = np.maximum(bins - F0, 0)
    for i in range(HALF):
        row = (even[i][:, None] * even_table).sum(0)[place] * live
        inner[i, :, 0] = row
        inner[i, :, 1] = row
        row = (odd[i][:, None] * odd_table).sum(0)[place] * live
        inner[HALF + i, :, 0] = -row
        inner[HALF + i, :, 1] = row
    outer = np.zeros((LAGS, RANK))
    for i in range(HALF):
        outer[MAXLAG:, i] = even[i]
        outer[MAXLAG::-1, i] = even[i]
        outer[MAXLAG + 1 :, HALF + i] = -odd[i]
        outer[MAXLAG - 1 :: -1, HALF + i] = odd[i]
    return outer, inner.reshape(RANK, FN).astype(np.float32)


def halves(value):
    high = value.astype(BF)
    low = (value - high.astype(F32)).astype(BF)
    return high, low


def dot(left, right):
    return jnp.dot(left, right, preferred_element_type=F32)


def spectrum_kernel(pairs_ref, count_ref, x_ref, first_ref, second_ref, out_ref, xs, ts, zs, ss):
    step = pl.program_id(0)

    @pl.when(step == 0)
    def _():
        xs[72:80, :] = jnp.zeros((8, xs.shape[1]), F32)

    flat = x_ref.reshape(QN * STEP, 128)
    for s in range(STEP):
        xs[0:QN, s * 128 : (s + 1) * 128] = flat[pl.ds(s, QN, stride=STEP), :]
    for pair in range(STEP // 2):
        high, low = halves(xs[:, pair * 256 : (pair + 1) * 256])
        both = dot(first_ref[...], jnp.concatenate([high, low], 0))
        section = both[: 2 * KPAD] + both[2 * KPAD :]
        for side in range(2):
            p = step * STEP + pair * 2 + side
            part = section[:, side * 128 : (side + 1) * 128]
            ts[pl.ds(p, KPAD, stride=2 * PN), :] = part[:KPAD]
            ts[pl.ds(PN + p, KPAD, stride=2 * PN), :] = part[KPAD:]

    @pl.when(step == pl.num_programs(0) - 1)
    def _():
        def residue(k, power):
            high, low = halves(ts[pl.ds(pl.multiple_of(k * 2 * PN, 2 * PN), 2 * PN), :])
            product = dot(second_ref[k], jnp.concatenate([high, low], 1))
            value = product[:GROUP, :128] + (product[:GROUP, 128:] + product[GROUP:, :128])
            zs[pl.ds(pl.multiple_of(k * GROUP, GROUP), GROUP), :] = value
            return power + jnp.sum(value * value, axis=0, keepdims=True)

        power = lax.fori_loop(0, KN, residue, jnp.zeros((1, 128), F32), unroll=2)
        factor = lax.rsqrt(power * (1.0 / NF) + EPSILON)
        out_ref[0:FN, :] = (zs[...] * factor).astype(BF)
        lane = lax.broadcasted_iota(jnp.int32, (8, 128), 1)
        sub = lax.broadcasted_iota(jnp.int32, (8, 128), 0)
        pick = jnp.where(lane == sub * (128 // VS), 1.0, 0.0).astype(BF)
        rows = lax.dot_general(
            pick, out_ref[0:FN, :], (((1,), (1,)), ((), ())), preferred_element_type=F32
        )
        ss[...] = jnp.zeros_like(ss)
        for j in range(VS):
            for c in range(CHUNKS):
                ss[j * SRC + c : j * SRC + c + 1, :] = rows[j : j + 1, c * 128 : (c + 1) * 128]
        owner = lax.axis_index("fibre")
        lane = lax.broadcasted_iota(jnp.int32, (1, 128), 1)
        table = jnp.where(lane == 2 * MAXP, count_ref[0], 0)
        for slot in range(MAXP):
            for side in range(2):
                offset = pairs_ref[slot * 2 + side] - owner
                table = jnp.where(lane == slot * 2 + side, offset, table)
        ss[TABLE - FN : TABLE - FN + 1, :] = table.astype(F32)
        out_ref[FN:ROWS, :] = ss[...].astype(BF)


def spectra(pair_blocks, pair_count, samples):
    smem = pl.BlockSpec(memory_space=pltpu.SMEM)
    first = jnp.asarray(first_matrix())
    second = jnp.asarray(second_matrix())
    return pl.pallas_call(
        spectrum_kernel,
        grid=(PN // STEP,),
        in_specs=[
            smem,
            smem,
            pl.BlockSpec((QN, STEP, 128), lambda g: (0, g, 0)),
            pl.BlockSpec(first.shape, lambda g: (0, 0)),
            pl.BlockSpec(second.shape, lambda g: (0, 0, 0)),
        ],
        out_specs=pl.BlockSpec((ROWS, 128), lambda g: (0, 0)),
        out_shape=jax.ShapeDtypeStruct((ROWS, 128), BF),
        scratch_shapes=[
            pltpu.VMEM((QPAD, STEP * 128), F32),
            pltpu.VMEM((KPAD * 2 * PN, 128), F32),
            pltpu.VMEM((FN, 128), F32),
            pltpu.VMEM((TAIL, 128), F32),
        ],
        compiler_params=pltpu.CompilerParams(vmem_limit_bytes=28 * 2**20),
        name="spectra",
    )(pair_blocks, pair_count, samples, first, second)


def pairs_kernel(b0, b1, b2, b3, b4, inner_ref, out_ref, receiver, source, weights):
    blocks = (b0, b1, b2, b3, b4)
    tail = b0[FN:ROWS, :].astype(F32)
    row = tail[TABLE - FN : TABLE - FN + 1, :].astype(jnp.int32)
    lane = lax.broadcasted_iota(jnp.int32, (1, 128), 1)

    def entry(index):
        return jnp.sum(jnp.where(lane == index, row, 0))

    count = entry(2 * MAXP)
    spot = lax.broadcasted_iota(jnp.int32, (TAIL, 128), 1)
    real_spot = lax.rem(spot, GROUP) < SLOT

    def one_pair(slot, carry):
        first = entry(2 * slot)
        second = entry(2 * slot + 1)
        for place, block in enumerate(blocks):

            @pl.when(second == place)
            def _():
                receiver[...] = block[0:FN, :]

            @pl.when(first == place)
            def _():
                source[...] = block[FN:ROWS, :].astype(F32)

        straight = source[...]
        crossed = jnp.where(
            real_spot, pltpu.roll(straight, 128 - SLOT, 1), pltpu.roll(straight, SLOT, 1)
        )
        for j in range(VS):
            for c in range(CHUNKS):
                at = j * SRC + c
                here = pl.ds(c * 128, 128)
                even = inner_ref[0:HALF, here] * straight[at : at + 1, :]
                odd = inner_ref[HALF:RANK, here] * crossed[at : at + 1, :]
                weights[j * RANK : j * RANK + HALF, here] = even.astype(BF)
                weights[j * RANK + HALF : (j + 1) * RANK, here] = odd.astype(BF)
        result = dot(weights[...], receiver[...]).astype(BF)
        for j in range(VS):
            out_ref[slot * VS + j] = result[j * RANK : (j + 1) * RANK]
        return carry

    def one_blank(slot, carry):
        for j in range(VS):
            out_ref[slot * VS + j] = jnp.zeros((RANK, 128), BF)
        return carry

    lax.fori_loop(0, count, one_pair, 0)
    lax.fori_loop(count, MAXP, one_blank, 0)


def pair_rows(blocks):
    _, inner = lag_factors()
    vmem = pl.BlockSpec(memory_space=pltpu.VMEM)
    return pl.pallas_call(
        pairs_kernel,
        in_specs=[vmem] * 6,
        out_specs=vmem,
        out_shape=jax.ShapeDtypeStruct((MAXP * VS, RANK, 128), BF),
        scratch_shapes=[
            pltpu.VMEM((FN, 128), BF),
            pltpu.VMEM((TAIL, 128), F32),
            pltpu.VMEM((VS * RANK, FN), BF),
        ],
        compiler_params=pltpu.CompilerParams(vmem_limit_bytes=28 * 2**20),
        name="pair_rows",
    )(*blocks, jnp.asarray(inner))


def lags_kernel(row_ref, outer_ref, out_ref):
    high, low = halves(row_ref[...])
    out_ref[...] = dot(outer_ref[...], jnp.concatenate([high, low, high], 0))


def lag_rows(row):
    outer, _ = lag_factors()
    high, low = split(outer * (1.0 / math.sqrt(NF * 8)))
    table = jnp.asarray(np.concatenate([high, high, low], 1))
    vmem = pl.BlockSpec(memory_space=pltpu.VMEM)
    return pl.pallas_call(
        lags_kernel,
        in_specs=[vmem, vmem],
        out_specs=vmem,
        out_shape=jax.ShapeDtypeStruct((LAGS, 128), F32),
        name="lag_rows",
    )(row, table)


def turned(array, by):
    size = lax.axis_size("fibre")
    return lax.ppermute(array, "fibre", [(i, (i + by) % size) for i in range(size)])


def shards(recordings, pair_blocks, pair_count):
    samples = recordings.reshape(QN, PN, 128)
    own = spectra(pair_blocks.reshape(2 * MAXP), pair_count, samples)
    middle = REACH // 2
    blocks = [own if d == middle else turned(own, middle - d) for d in range(REACH + 1)]
    rows = pair_rows(blocks)
    shared = lax.all_to_all(rows, "tm", 0, 0)
    row = jnp.sum(shared.astype(F32), axis=0)
    return lag_rows(turned(row, -middle))[None, None]


def solution(mesh):
    in_specs = (P("tm", "fibre", None, None), P("fibre", None, None), P("fibre"))
    out_specs = P("fibre", "tm", None, None)
    return jax.shard_map(shards, mesh=mesh, in_specs=in_specs, out_specs=out_specs, check_vma=False)
```

time: 248 us -> 90.2 us (0.36)
  the two profiles are of different devices: /device:TPU:2 before, /device:TPU:1 now
where the time goes in v1:
time: 90.2 us; the launch traced here: 89.8 us
  waiting for transfers between devices  25.5 us (28%)
  starting transfers between devices  24.3 us (27%)
  blocking collectives  17.4 us (19%)
  Pallas kernels  14 us (16%)
  local copies, waits for them, and re-layouts  7.77 us (9%)
    ppermute x5, waiting for transfers between devices, turned(): lax.ppermute(array, 'fibre', [(i, (i + by) % size) for i in range(size)])  25.5 us
    ppermute x5, starting transfers between devices, turned(): lax.ppermute(array, 'fibre', [(i, (i + by) % size) for i in range(size)])  24.3 us
    all_to_all x1, blocking collectives, shards(): shared = lax.all_to_all(rows, 'tm', 0, 0)  17.4 us
    pallas_call x1, Pallas kernels, spectra(): pl.pallas_call(spectrum_kernel, grid=(PN // STEP,), in_specs=[smem, smem,...  8.01 us
    unnamed x11, local copies, waits for them, and re-layouts  5.87 us
    pallas_call x1, Pallas kernels, pair_rows(): pl.pallas_call(pairs_kernel, in_specs=[vmem] * 6, out_specs=vmem, out_sha...  3.97 us
    pallas_call x1, Pallas kernels, lag_rows(): pl.pallas_call(lags_kernel, in_specs=[vmem, vmem], out_specs=vmem, out_sh...  2.07 us
    broadcast_in_dim x1, local copies, waits for them, and re-layouts, shards(): return lag_rows(turned(row, -middle))[None, None]  1.82 us
  transfers between devices with their start and end apart: 5, of which 4 were waited for; matrix products, arithmetic and copies ran while one was open for 0% of the time, Pallas kernels for 0%

profile of v1, /device:TPU:1, one launch (start us, length us, event | category | flops | bytes accessed | tf_op | source)
XLA Modules:
  0.0 89.8 jit_solution(3880932647663200985)
XLA Ops:
  0.7 0.8 copy.10
  1.4 0.1 reshape.6.pairs_ref
  1.5 0.0 copy-start
  1.5 1.9 %copy-done = f32[1,1,6000,128]{3,2,1,0:T(8,128)S(1)} copy-done((f32[1,1,6000,128]{3,2,1,0:T(8,128)S(1)}, f32[1,1,6000,128]{3,2,1,0:T(8,128)}, u32[]{:S(2)}) %copy-start) | copy-done | bytes 3072024
  3.4 1.7 %copy-done.1 = bf16[38,128,160]{2,1,0:T(8,128)(2,1)S(1)} copy-done((bf16[38,128,160]{2,1,0:T(8,128)(2,1)S(1)}, bf16[38,128,160]{2,1,0:T(8,128)(2,1)}, u32[]{:S(2)}) %copy-start.1) | copy-done | bytes 1556504
  5.1 0.9 copy-done.3
  6.0 8.0 %spectra.1.b2 = bf16[2480,128]{1,0:T(8,128)(2,1)S(1)} custom-call(s32[8]{0:T(128)S(1)} %reshape.6.pairs_ref, s32[1]{0:T(128)S(6)} %copy.12.count_ref, f32[75,80,128]{2,1,0:T(8,128)S(1)} %bitcast.2, bf16[160,160]{1,0:T(8,128)(2,1)S(1)} %copy-done.3, bf16[38,128,160]{2,1,0:T(8,128)(2,1)S(1)} %copy-done.1), custom_call_target="tpu_custom_call" | custom-call | tf_op jit(solution)/shard_map/spectra/pallas_call | solution.py:223
  14.0 13.7 %collective-permute-start.3 = (bf16[2480,128]{1,0:T(8,128)(2,1)S(1)}, bf16[2480,128]{1,0:T(8,128)(2,1)S(1)}, u32[]{:S(2)}, u32[]{:S(2)}) collective-permute-start(bf16[2480,128]{1,0:T(8,128)(2,1)S(1)} %spectra.1.b2), channel_id=1, source_target_pairs={{0,496},{8,504},{16,0},{24,8},{32,16},{40,24},{48,32},{56,40},{64,... | collective-permute-start | bytes 1904648 | tf_op jit(solution)/shard_map/ppermute | solution.py:337
  27.7 2.9 %collective-permute-start.2 = (bf16[2480,128]{1,0:T(8,128)(2,1)S(1)}, bf16[2480,128]{1,0:T(8,128)(2,1)S(1)}, u32[]{:S(2)}, u32[]{:S(2)}) collective-permute-start(bf16[2480,128]{1,0:T(8,128)(2,1)S(1)} %spectra.1.b2), channel_id=1, source_target_pairs={{0,504},{8,0},{16,8},{24,16},{32,24},{40,32},{48,40},{56,48},{64,5... | collective-permute-start | bytes 1904648 | tf_op jit(solution)/shard_map/ppermute | solution.py:337
  30.5 2.7 %collective-permute-start.1 = (bf16[2480,128]{1,0:T(8,128)(2,1)S(1)}, bf16[2480,128]{1,0:T(8,128)(2,1)S(1)}, u32[]{:S(2)}, u32[]{:S(2)}) collective-permute-start(bf16[2480,128]{1,0:T(8,128)(2,1)S(1)} %spectra.1.b2), channel_id=1, source_target_pairs={{0,8},{8,16},{16,24},{24,32},{32,40},{40,48},{48,56},{56,64},{64,7... | collective-permute-start | bytes 1904648 | tf_op jit(solution)/shard_map/ppermute | solution.py:337
  33.2 1.9 %collective-permute-start = (bf16[2480,128]{1,0:T(8,128)(2,1)S(1)}, bf16[2480,128]{1,0:T(8,128)(2,1)S(1)}, u32[]{:S(2)}, u32[]{:S(2)}) collective-permute-start(bf16[2480,128]{1,0:T(8,128)(2,1)S(1)} %spectra.1.b2), channel_id=1, source_target_pairs={{0,16},{8,24},{16,32},{24,40},{32,48},{40,56},{48,64},{56,72},{64,... | collective-permute-start | bytes 1904648 | tf_op jit(solution)/shard_map/ppermute | solution.py:337
  35.2 5.4 %collective-permute-done.3.b4 = bf16[2480,128]{1,0:T(8,128)(2,1)S(1)} collective-permute-done((bf16[2480,128]{1,0:T(8,128)(2,1)S(1)}, bf16[2480,128]{1,0:T(8,128)(2,1)S(1)}, u32[]{:S(2)}, u32[]{:S(2)}) %collective-permute-start.3) | collective-permute-done | bytes 634912 | tf_op jit(solution)/shard_map/ppermute | solution.py:337
  40.6 0.0 collective-permute-done.2.b3
  40.6 4.2 %collective-permute-done.1.b1 = bf16[2480,128]{1,0:T(8,128)(2,1)S(1)} collective-permute-done((bf16[2480,128]{1,0:T(8,128)(2,1)S(1)}, bf16[2480,128]{1,0:T(8,128)(2,1)S(1)}, u32[]{:S(2)}, u32[]{:S(2)}) %collective-permute-start.1) | collective-permute-done | bytes 634912 | tf_op jit(solution)/shard_map/ppermute | solution.py:337
  44.8 13.7 %collective-permute-done.b0 = bf16[2480,128]{1,0:T(8,128)(2,1)S(1)} collective-permute-done((bf16[2480,128]{1,0:T(8,128)(2,1)S(1)}, bf16[2480,128]{1,0:T(8,128)(2,1)S(1)}, u32[]{:S(2)}, u32[]{:S(2)}) %collective-permute-start) | collective-permute-done | bytes 634912 | tf_op jit(solution)/shard_map/ppermute | solution.py:337
  58.5 0.0 copy-done.2
  58.5 4.0 %pair_rows.1 = bf16[8,192,128]{2,1,0:T(8,128)(2,1)S(1)} custom-call(bf16[2480,128]{1,0:T(8,128)(2,1)S(1)} %collective-permute-done.b0, bf16[2480,128]{1,0:T(8,128)(2,1)S(1)} %collective-permute-done.1.b1, bf16[2480,128]{1,0:T(8,128)(2,1)S(1)} %spectra.1.b2, bf16[2480,128]{1,0:T(8,128)(2,1)S(1)} %collective-permute-done.2.b3, ...), custom_call_target="tpu_custom_call" | custom-call | tf_op jit(solution)/shard_map/pair_rows/pallas_call | solution.py:301
  62.5 17.4 %all_to_all.5 = bf16[8,192,128]{2,1,0:T(8,128)(2,1)S(1)} all-to-all(bf16[8,192,128]{2,1,0:T(8,128)(2,1)S(1)} %pair_rows.1), channel_id=1, replica_groups=mesh['fibre'=64,'tm'=8] {'tm'}, dimensions={0} | all-to-all | bytes 786432 | tf_op jit(solution)/shard_map/all_to_all | solution.py:346
  79.8 0.1 convert_reduce_fusion
  79.9 3.1 %collective-permute-start.4 = (f32[192,128]{1,0:T(8,128)S(1)}, f32[192,128]{1,0:T(8,128)S(1)}, u32[]{:S(2)}, u32[]{:S(2)}) collective-permute-start(f32[192,128]{1,0:T(8,128)S(1)} %convert_reduce_fusion), channel_id=1, source_target_pairs={{0,496},{8,504},{16,0},{24,8},{32,16},{40,24},{48,32},{56,40},{64,... | collective-permute-start | bytes 294920 | tf_op jit(solution)/shard_map/ppermute | solution.py:337
  83.0 2.2 %collective-permute-done.4.row_ref = f32[192,128]{1,0:T(8,128)S(1)} collective-permute-done((f32[192,128]{1,0:T(8,128)S(1)}, f32[192,128]{1,0:T(8,128)S(1)}, u32[]{:S(2)}, u32[]{:S(2)}) %collective-permute-start.4) | collective-permute-done | bytes 98336 | tf_op jit(solution)/shard_map/ppermute | solution.py:337
  85.3 0.6 copy-done.4
  85.9 2.1 %lag_rows.1 = f32[401,128]{1,0:T(8,128)} custom-call(f32[192,128]{1,0:T(8,128)} %copy-done.4, bf16[401,576]{1,0:T(8,128)(2,1)} %constant.13.clone.outer_ref), custom_call_target="tpu_custom_call" | custom-call | tf_op jit(solution)/shard_map/lag_rows/pallas_call | solution.py:326
  88.0 1.8 %copy.11 = f32[1,1,401,128]{3,1,2,0:T(1,128)} copy(f32[1,1,401,128]{3,2,1,0:T(8,128)} %bitcast.3) | data formatting | bytes 410624 | tf_op jit(solution)/shard_map/broadcast_in_dim | solution.py:348
  (4 shorter events, 0.0 us)
Async XLA Ops:
  1.5 1.9 %copy-start = (f32[1,1,6000,128]{3,2,1,0:T(8,128)S(1)}, f32[1,1,6000,128]{3,2,1,0:T(8,128)}, u32[]{:S(2)}) copy-start(f32[1,1,6000,128]{3,2,1,0:T(8,128)} %param.7) | copy-start | bytes 9216004
  3.4 1.7 %copy-start.1 = (bf16[38,128,160]{2,1,0:T(8,128)(2,1)S(1)}, bf16[38,128,160]{2,1,0:T(8,128)(2,1)}, u32[]{:S(2)}) copy-start(bf16[38,128,160]{2,1,0:T(8,128)(2,1)} %constant.11.clone.second_ref) | copy-start | bytes 4669444
  5.1 0.9 copy-start.3
  6.0 52.5 %copy-start.2 = (f32[192,2432]{1,0:T(8,128)S(1)}, f32[192,2432]{1,0:T(8,128)}, u32[]{:S(2)}) copy-start(f32[192,2432]{1,0:T(8,128)} %constant.12.clone.inner_ref) | copy-start | bytes 5603332
  14.0 26.6 %collective-permute-start.3 = (bf16[2480,128]{1,0:T(8,128)(2,1)S(1)}, bf16[2480,128]{1,0:T(8,128)(2,1)S(1)}, u32[]{:S(2)}, u32[]{:S(2)}) collective-permute-start(bf16[2480,128]{1,0:T(8,128)(2,1)S(1)} %spectra.1.b2), channel_id=1, source_target_pairs={{0,496},{8,504},{16,0},{24,8},{32,16},{40,24},{48,32},{56,40},{64,... | collective-permute-start | bytes 1904648 | tf_op jit(solution)/shard_map/ppermute | solution.py:337
  27.7 12.9 %collective-permute-start.2 = (bf16[2480,128]{1,0:T(8,128)(2,1)S(1)}, bf16[2480,128]{1,0:T(8,128)(2,1)S(1)}, u32[]{:S(2)}, u32[]{:S(2)}) collective-permute-start(bf16[2480,128]{1,0:T(8,128)(2,1)S(1)} %spectra.1.b2), channel_id=1, source_target_pairs={{0,504},{8,0},{16,8},{24,16},{32,24},{40,32},{48,40},{56,48},{64,5... | collective-permute-start | bytes 1904648 | tf_op jit(solution)/shard_map/ppermute | solution.py:337
  30.5 14.2 %collective-permute-start.1 = (bf16[2480,128]{1,0:T(8,128)(2,1)S(1)}, bf16[2480,128]{1,0:T(8,128)(2,1)S(1)}, u32[]{:S(2)}, u32[]{:S(2)}) collective-permute-start(bf16[2480,128]{1,0:T(8,128)(2,1)S(1)} %spectra.1.b2), channel_id=1, source_target_pairs={{0,8},{8,16},{16,24},{24,32},{32,40},{40,48},{48,56},{56,64},{64,7... | collective-permute-start | bytes 1904648 | tf_op jit(solution)/shard_map/ppermute | solution.py:337
  33.2 25.2 %collective-permute-start = (bf16[2480,128]{1,0:T(8,128)(2,1)S(1)}, bf16[2480,128]{1,0:T(8,128)(2,1)S(1)}, u32[]{:S(2)}, u32[]{:S(2)}) collective-permute-start(bf16[2480,128]{1,0:T(8,128)(2,1)S(1)} %spectra.1.b2), channel_id=1, source_target_pairs={{0,16},{8,24},{16,32},{24,40},{32,48},{40,56},{48,64},{56,72},{64,... | collective-permute-start | bytes 1904648 | tf_op jit(solution)/shard_map/ppermute | solution.py:337
  79.9 5.4 %collective-permute-start.4 = (f32[192,128]{1,0:T(8,128)S(1)}, f32[192,128]{1,0:T(8,128)S(1)}, u32[]{:S(2)}, u32[]{:S(2)}) collective-permute-start(f32[192,128]{1,0:T(8,128)S(1)} %convert_reduce_fusion), channel_id=1, source_target_pairs={{0,496},{8,504},{16,0},{24,8},{32,16},{40,24},{48,32},{56,40},{64,... | collective-permute-start | bytes 294920 | tf_op jit(solution)/shard_map/ppermute | solution.py:337
  85.2 0.6 copy-start.4

commit v2 on v1

--- a/solution.py
+++ b/solution.py
@@ -35,6 +35,9 @@
 HALF = 96
 RANK = 2 * HALF
 STEP = 16
+STEPS = PN // STEP
+UNROLL = 19
+FRONT_VMEM = 28 * 2**20
 BF = jnp.bfloat16
 F32 = jnp.float32
 
@@ -163,84 +166,105 @@
     return jnp.dot(left, right, preferred_element_type=F32)
 
 
-def spectrum_kernel(pairs_ref, count_ref, x_ref, first_ref, second_ref, out_ref, xs, ts, zs, ss):
-    step = pl.program_id(0)
-
-    @pl.when(step == 0)
-    def _():
-        xs[72:80, :] = jnp.zeros((8, xs.shape[1]), F32)
-
-    flat = x_ref.reshape(QN * STEP, 128)
-    for s in range(STEP):
-        xs[0:QN, s * 128 : (s + 1) * 128] = flat[pl.ds(s, QN, stride=STEP), :]
-    for pair in range(STEP // 2):
-        high, low = halves(xs[:, pair * 256 : (pair + 1) * 256])
-        both = dot(first_ref[...], jnp.concatenate([high, low], 0))
-        section = both[: 2 * KPAD] + both[2 * KPAD :]
+def spectrum_kernel(
+    pairs_ref, count_ref, x_hbm, first_hbm, second_hbm, out_ref,
+    xs, first, second, pad, ts, zs, ss, sems,
+):
+    def load(g):
+        return pltpu.make_async_copy(
+            x_hbm.at[:, pl.ds(g * STEP, STEP), :], xs.at[g], sems.at[g]
+        )
+
+    first_copy = pltpu.make_async_copy(first_hbm, first, sems.at[STEPS])
+    second_copy = pltpu.make_async_copy(second_hbm, second, sems.at[STEPS + 1])
+    first_copy.start()
+    for g in range(STEPS):
+        load(g).start()
+    second_copy.start()
+    pad[72:80, :] = jnp.zeros((8, STEP * 128), F32)
+
+    def sections(g, carry):
+        load(g).wait()
+        flat = xs.at[g].reshape(QN * STEP, 128)
+        for s in range(STEP):
+            pad[0:QN, s * 128 : (s + 1) * 128] = flat[pl.ds(s, QN, stride=STEP), :]
+        for pair in range(STEP // 2):
+            high, low = halves(pad[:, pair * 256 : (pair + 1) * 256])
+            both = dot(first[...], jnp.concatenate([high, low], 0))
+            section = both[: 2 * KPAD] + both[2 * KPAD :]
+            for side in range(2):
+                p = g * STEP + pair * 2 + side
+                part = section[:, side * 128 : (side + 1) * 128]
+                ts[pl.ds(p, KPAD, stride=2 * PN), :] = part[:KPAD]
+                ts[pl.ds(PN + p, KPAD, stride=2 * PN), :] = part[KPAD:]
+        return carry
+
+    first_copy.wait()
+    lax.fori_loop(0, STEPS, sections, 0)
+    second_copy.wait()
+
+    def residue(k, power):
+        high, low = halves(ts[pl.ds(pl.multiple_of(k * 2 * PN, 2 * PN), 2 * PN), :])
+        product = dot(second[k], jnp.concatenate([high, low], 1))
+        value = product[:GROUP, :128] + (product[:GROUP, 128:] + product[GROUP:, :128])
+        zs[pl.ds(pl.multiple_of(k * GROUP, GROUP), GROUP), :] = value
+        return power + jnp.sum((value * value).reshape(GROUP // 8, 8, 128), axis=0)
+
+    power = lax.fori_loop(0, KN, residue, jnp.zeros((8, 128), F32), unroll=UNROLL)
+    power = jnp.sum(power, axis=0, keepdims=True)
+    factor = lax.rsqrt(power * (1.0 / NF) + EPSILON)
+    out_ref[0:FN, :] = (zs[...] * factor).astype(BF)
+    lane = lax.broadcasted_iota(jnp.int32, (8, 128), 1)
+    sub = lax.broadcasted_iota(jnp.int32, (8, 128), 0)
+    pick = jnp.where(lane == sub * (128 // VS), 1.0, 0.0).astype(BF)
+    rows = lax.dot_general(
+        pick, out_ref[0:FN, :], (((1,), (1,)), ((), ())), preferred_element_type=F32
+    )
+    ss[...] = jnp.zeros_like(ss)
+    for j in range(VS):
+        for c in range(CHUNKS):
+            ss[j * SRC + c : j * SRC + c + 1, :] = rows[j : j + 1, c * 128 : (c + 1) * 128]
+    owner = lax.axis_index("fibre")
+    lane = lax.broadcasted_iota(jnp.int32, (1, 128), 1)
+    table = jnp.where(lane == 2 * MAXP, count_ref[0], 0)
+    for slot in range(MAXP):
         for side in range(2):
-            p = step * STEP + pair * 2 + side
-            part = section[:, side * 128 : (side + 1) * 128]
-            ts[pl.ds(p, KPAD, stride=2 * PN), :] = part[:KPAD]
-            ts[pl.ds(PN + p, KPAD, stride=2 * PN), :] = part[KPAD:]
-
-    @pl.when(step == pl.num_programs(0) - 1)
-    def _():
-        def residue(k, power):
-            high, low = halves(ts[pl.ds(pl.multiple_of(k * 2 * PN, 2 * PN), 2 * PN), :])
-            product = dot(second_ref[k], jnp.concatenate([high, low], 1))
-            value = product[:GROUP, :128] + (product[:GROUP, 128:] + product[GROUP:, :128])
-            zs[pl.ds(pl.multiple_of(k * GROUP, GROUP), GROUP), :] = value
-            return power + jnp.sum(value * value, axis=0, keepdims=True)
-
-        power = lax.fori_loop(0, KN, residue, jnp.zeros((1, 128), F32), unroll=2)
-        factor = lax.rsqrt(power * (1.0 / NF) + EPSILON)
-        out_ref[0:FN, :] = (zs[...] * factor).astype(BF)
-        lane = lax.broadcasted_iota(jnp.int32, (8, 128), 1)
-        sub = lax.broadcasted_iota(jnp.int32, (8, 128), 0)
-        pick = jnp.where(lane == sub * (128 // VS), 1.0, 0.0).astype(BF)
-        rows = lax.dot_general(
-            pick, out_ref[0:FN, :], (((1,), (1,)), ((), ())), preferred_element_type=F32
-        )
-        ss[...] = jnp.zeros_like(ss)
-        for j in range(VS):
-            for c in range(CHUNKS):
-                ss[j * SRC + c : j * SRC + c + 1, :] = rows[j : j + 1, c * 128 : (c + 1) * 128]
-        owner = lax.axis_index("fibre")
-        lane = lax.broadcasted_iota(jnp.int32, (1, 128), 1)
-        table = jnp.where(lane == 2 * MAXP, count_ref[0], 0)
-        for slot in range(MAXP):
-            for side in range(2):
-                offset = pairs_ref[slot * 2 + side] - owner
-                table = jnp.where(lane == slot * 2 + side, offset, table)
-        ss[TABLE - FN : TABLE - FN + 1, :] = table.astype(F32)
-        out_ref[FN:ROWS, :] = ss[...].astype(BF)
+            offset = pairs_ref[side, slot] - owner
+            table = jnp.where(lane == slot * 2 + side, offset, table)
+    ss[TABLE - FN : TABLE - FN + 1, :] = table.astype(F32)
+    out_ref[FN:ROWS, :] = ss[...].astype(BF)
+
+
+def in_hbm(array):
+    return pltpu.with_memory_space_constraint(array, pltpu.HBM)
 
 
 def spectra(pair_blocks, pair_count, samples):
     smem = pl.BlockSpec(memory_space=pltpu.SMEM)
+    vmem = pl.BlockSpec(memory_space=pltpu.VMEM)
+    hbm = pl.BlockSpec(memory_space=pltpu.HBM)
     first = jnp.asarray(first_matrix())
     second = jnp.asarray(second_matrix())
     return pl.pallas_call(
         spectrum_kernel,
-        grid=(PN // STEP,),
-        in_specs=[
-            smem,
-            smem,
-            pl.BlockSpec((QN, STEP, 128), lambda g: (0, g, 0)),
-            pl.BlockSpec(first.shape, lambda g: (0, 0)),
-            pl.BlockSpec(second.shape, lambda g: (0, 0, 0)),
-        ],
-        out_specs=pl.BlockSpec((ROWS, 128), lambda g: (0, 0)),
+        in_specs=[smem, smem, hbm, hbm, hbm],
+        out_specs=vmem,
         out_shape=jax.ShapeDtypeStruct((ROWS, 128), BF),
         scratch_shapes=[
+            pltpu.VMEM((STEPS, QN, STEP, 128), F32),
+            pltpu.VMEM(first.shape, BF),
+            pltpu.VMEM(second.shape, BF),
             pltpu.VMEM((QPAD, STEP * 128), F32),
             pltpu.VMEM((KPAD * 2 * PN, 128), F32),
             pltpu.VMEM((FN, 128), F32),
             pltpu.VMEM((TAIL, 128), F32),
+            pltpu.SemaphoreType.DMA((STEPS + 2,)),
         ],
-        compiler_params=pltpu.CompilerParams(vmem_limit_bytes=28 * 2**20),
+        compiler_params=pltpu.CompilerParams(vmem_limit_bytes=FRONT_VMEM),
         name="spectra",
-    )(pair_blocks, pair_count, samples, first, second)
+    )(
+        in_hbm(pair_blocks), pair_count, in_hbm(samples), in_hbm(first), in_hbm(second)
+    )
 
 
 def pairs_kernel(b0, b1, b2, b3, b4, inner_ref, out_ref, receiver, source, weights):
@@ -252,13 +276,18 @@
     def entry(index):
         return jnp.sum(jnp.where(lane == index, row, 0))
 
+    even = lax.rem(lax.axis_index("fibre"), 2) == 0
+
+    def place_of(offset):
+        return jnp.where(even & (lax.rem(offset, 2) == 1), REACH - offset, offset)
+
     count = entry(2 * MAXP)
     spot = lax.broadcasted_iota(jnp.int32, (TAIL, 128), 1)
     real_spot = lax.rem(spot, GROUP) < SLOT
 
     def one_pair(slot, carry):
-        first = entry(2 * slot)
-        second = entry(2 * slot + 1)
+        first = place_of(entry(2 * slot))
+        second = place_of(entry(2 * slot + 1))
         for place, block in enumerate(blocks):
 
             @pl.when(second == place)
@@ -315,7 +344,7 @@
 
 def lags_kernel(row_ref, outer_ref, out_ref):
     high, low = halves(row_ref[...])
-    out_ref[...] = dot(outer_ref[...], jnp.concatenate([high, low, high], 0))
+    out_ref[:, 0, :] = dot(outer_ref[...], jnp.concatenate([high, low, high], 0))
 
 
 def lag_rows(row):
@@ -327,7 +356,8 @@
         lags_kernel,
         in_specs=[vmem, vmem],
         out_specs=vmem,
-        out_shape=jax.ShapeDtypeStruct((LAGS, 128), F32),
+        out_shape=jax.ShapeDtypeStruct((LAGS, 1, 128), F32),
+        compiler_params=pltpu.CompilerParams(vmem_limit_bytes=8 * 2**20),
         name="lag_rows",
     )(row, table)
 
@@ -337,15 +367,27 @@
     return lax.ppermute(array, "fibre", [(i, (i + by) % size) for i in range(size)])
 
 
+def swapped(array):
+    size = lax.axis_size("fibre")
+    return lax.ppermute(array, "fibre", [(i, i ^ 1) for i in range(size)])
+
+
+def gathered(own):
+    even = lax.axis_index("fibre") % 2 == 0
+    ahead = turned(own, -2)
+    behind = turned(own, 2)
+    sibling = swapped(own)
+    other = swapped(jnp.where(even, ahead, behind))
+    return [behind, sibling, own, other, ahead]
+
+
 def shards(recordings, pair_blocks, pair_count):
     samples = recordings.reshape(QN, PN, 128)
-    own = spectra(pair_blocks.reshape(2 * MAXP), pair_count, samples)
-    middle = REACH // 2
-    blocks = [own if d == middle else turned(own, middle - d) for d in range(REACH + 1)]
-    rows = pair_rows(blocks)
+    own = spectra(pair_blocks[0].T, pair_count, samples)
+    rows = pair_rows(gathered(own))
     shared = lax.all_to_all(rows, "tm", 0, 0)
     row = jnp.sum(shared.astype(F32), axis=0)
-    return lag_rows(turned(row, -middle))[None, None]
+    return lag_rows(turned(row, -2))[None].transpose(0, 2, 1, 3)
 
 
 def solution(mesh):

time: 90.2 us -> 73.7 us (0.82)
  waiting for transfers between devices: 25.5 us -> 13.3 us
  local copies, waits for them, and re-layouts: 7.77 us -> 0.01 us
  Pallas kernels: 14 us -> 8.51 us
  starting transfers between devices: 24.3 us -> 29.5 us
  blocking collectives: 17.4 us -> 20.5 us
    ppermute x5 -> x3, waiting for transfers between devices: 25.5 us -> 11.7 us  [turned(): lax.ppermute(array, 'fibre', [(i, (i + by) % size) for i in range(size)])]
    ppermute x0 -> x2, starting transfers between devices: none -> 6.45 us  [swapped(): return lax.ppermute(array, 'fibre', [(i, i ^ 1) for i in range(size)])]
    unnamed x11 -> x4, local copies, waits for them, and re-layouts: 5.87 us -> 0.01 us
    all_to_all x1, blocking collectives: 17.4 us -> 20.5 us  [shards(): shared = lax.all_to_all(rows, 'tm', 0, 0)]
    pallas_call x1, Pallas kernels: 3.97 us -> 1.08 us  [pair_rows(): pl.pallas_call(pairs_kernel, in_specs=[vmem] * 6, out_specs=vmem, out_sha...]
    broadcast_in_dim x1 -> x0, local copies, waits for them, and re-layouts: 1.82 us -> none  [shards(): return lag_rows(turned(row, -middle))[None, None]]
    ppermute x0 -> x2, waiting for transfers between devices: none -> 1.67 us  [swapped(): return lax.ppermute(array, 'fibre', [(i, i ^ 1) for i in range(size)])]
    pallas_call x1, Pallas kernels: 8.01 us -> 6.36 us  [spectra(): pl.pallas_call(spectrum_kernel, in_specs=[smem, smem, hbm, hbm, hbm], out...]
where the time goes in v2:
time: 73.7 us; the launch traced here: 72.7 us
  starting transfers between devices  29.5 us (40%)
  blocking collectives  20.5 us (28%)
  waiting for transfers between devices  13.3 us (18%)
  Pallas kernels  8.51 us (12%)
  between operations  0.75 us (1%)
    ppermute x3, starting transfers between devices, turned(): lax.ppermute(array, 'fibre', [(i, (i + by) % size) for i in range(size)])  23 us
    all_to_all x1, blocking collectives, shards(): shared = lax.all_to_all(rows, 'tm', 0, 0)  20.5 us
    ppermute x3, waiting for transfers between devices, turned(): lax.ppermute(array, 'fibre', [(i, (i + by) % size) for i in range(size)])  11.7 us
    ppermute x2, starting transfers between devices, swapped(): return lax.ppermute(array, 'fibre', [(i, i ^ 1) for i in range(size)])  6.45 us
    pallas_call x1, Pallas kernels, spectra(): pl.pallas_call(spectrum_kernel, in_specs=[smem, smem, hbm, hbm, hbm], out...  6.36 us
    ppermute x2, waiting for transfers between devices, swapped(): return lax.ppermute(array, 'fibre', [(i, i ^ 1) for i in range(size)])  1.67 us
  transfers between devices with their start and end apart: 5, of which 4 were waited for; matrix products, arithmetic and copies ran while one was open for 0% of the time, Pallas kernels for 0%

profile of v2, /device:TPU:1, one launch (start us, length us, event | category | flops | bytes accessed | tf_op | source)
XLA Modules:
  0.0 72.7 jit_solution(16839991975921487786)
XLA Ops:
  0.7 6.4 %spectra.1.b2 = bf16[2480,128]{1,0:T(8,128)(2,1)S(1)} custom-call(s32[2,4]{1,0:T(2,128)} %bitcast.8, s32[1]{0:T(128)S(6)} %copy.9.count_ref, f32[75,80,128]{2,1,0:T(8,128)} %bitcast.7, bf16[160,160]{1,0:T(8,128)(2,1)} %constant.30.clone.first_hbm, bf16[38,128,160]{2,1,0:T(8,128)(2,1)} %constant.31.clone.second_hbm), custom_call_target="tpu_custom_call" | custom-call | tf_op jit(solution)/shard_map/spectra/pallas_call | solution.py:248
  7.0 4.8 %collective-permute-start = (bf16[2480,128]{1,0:T(8,128)(2,1)S(1)}, bf16[2480,128]{1,0:T(8,128)(2,1)S(1)}, u32[]{:S(2)}, u32[]{:S(2)}) collective-permute-start(bf16[2480,128]{1,0:T(8,128)(2,1)S(1)} %spectra.1.b2), channel_id=1, source_target_pairs={{0,16},{8,24},{16,32},{24,40},{32,48},{40,56},{48,64},{56,72},{64,... | collective-permute-start | bytes 1904648 | tf_op jit(solution)/shard_map/ppermute | solution.py:367
  11.9 10.8 %collective-permute-start.2 = (bf16[2480,128]{1,0:T(8,128)(2,1)S(1)}, bf16[2480,128]{1,0:T(8,128)(2,1)S(1)}, u32[]{:S(2)}, u32[]{:S(2)}) collective-permute-start(bf16[2480,128]{1,0:T(8,128)(2,1)S(1)} %spectra.1.b2), channel_id=1, source_target_pairs={{0,496},{8,504},{16,0},{24,8},{32,16},{40,24},{48,32},{56,40},{64,... | collective-permute-start | bytes 1904648 | tf_op jit(solution)/shard_map/ppermute | solution.py:367
  22.7 2.9 %collective-permute-start.1 = (bf16[2480,128]{1,0:T(8,128)(2,1)S(1)}, bf16[2480,128]{1,0:T(8,128)(2,1)S(1)}, u32[]{:S(2)}, u32[]{:S(2)}) collective-permute-start(bf16[2480,128]{1,0:T(8,128)(2,1)S(1)} %spectra.1.b2), channel_id=1, source_target_pairs={{0,8},{8,0},{16,24},{24,16},{32,40},{40,32},{48,56},{56,48},{64,72... | collective-permute-start | bytes 1904648 | tf_op jit(solution)/shard_map/ppermute | solution.py:372
  25.5 0.0 copy-start
  25.5 9.2 %collective-permute-done.b0 = bf16[2480,128]{1,0:T(8,128)(2,1)S(1)} collective-permute-done((bf16[2480,128]{1,0:T(8,128)(2,1)S(1)}, bf16[2480,128]{1,0:T(8,128)(2,1)S(1)}, u32[]{:S(2)}, u32[]{:S(2)}) %collective-permute-start) | collective-permute-done | bytes 634912 | tf_op jit(solution)/shard_map/ppermute | solution.py:367
  34.7 0.9 %collective-permute-done.2.b4 = bf16[2480,128]{1,0:T(8,128)(2,1)S(1)} collective-permute-done((bf16[2480,128]{1,0:T(8,128)(2,1)S(1)}, bf16[2480,128]{1,0:T(8,128)(2,1)S(1)}, u32[]{:S(2)}, u32[]{:S(2)}) %collective-permute-start.2) | collective-permute-done | bytes 634912 | tf_op jit(solution)/shard_map/ppermute | solution.py:367
  35.6 0.1 broadcast_select_fusion
  35.7 0.0 copy-start.1
  35.7 3.6 %collective-permute-start.3 = (bf16[2480,128]{1,0:T(8,128)(2,1)S(1)}, bf16[2480,128]{1,0:T(8,128)(2,1)S(1)}, u32[]{:S(2)}, u32[]{:S(2)}) collective-permute-start(bf16[2480,128]{1,0:T(8,128)(2,1)S(1)} %broadcast_select_fusion), channel_id=1, source_target_pairs={{0,8},{8,0},{16,24},{24,16},{32,40},{40,32},{48,56},{56,48},{64,72... | collective-permute-start | bytes 1904648 | tf_op jit(solution)/shard_map/ppermute | solution.py:372
  39.3 0.0 collective-permute-done.1.b1
  39.3 1.7 %collective-permute-done.3.b3 = bf16[2480,128]{1,0:T(8,128)(2,1)S(1)} collective-permute-done((bf16[2480,128]{1,0:T(8,128)(2,1)S(1)}, bf16[2480,128]{1,0:T(8,128)(2,1)S(1)}, u32[]{:S(2)}, u32[]{:S(2)}) %collective-permute-start.3) | collective-permute-done | bytes 634912 | tf_op jit(solution)/shard_map/ppermute | solution.py:372
  41.0 0.0 copy-done
  41.0 1.1 %pair_rows.1 = bf16[8,192,128]{2,1,0:T(8,128)(2,1)S(1)} custom-call(bf16[2480,128]{1,0:T(8,128)(2,1)S(1)} %collective-permute-done.b0, bf16[2480,128]{1,0:T(8,128)(2,1)S(1)} %collective-permute-done.1.b1, bf16[2480,128]{1,0:T(8,128)(2,1)S(1)} %spectra.1.b2, bf16[2480,128]{1,0:T(8,128)(2,1)S(1)} %collective-permute-done.3.b3, ...), custom_call_target="tpu_custom_call" | custom-call | tf_op jit(solution)/shard_map/pair_rows/pallas_call | solution.py:330
  42.1 20.5 %all_to_all.5 = bf16[8,192,128]{2,1,0:T(8,128)(2,1)S(1)} all-to-all(bf16[8,192,128]{2,1,0:T(8,128)(2,1)S(1)} %pair_rows.1), channel_id=1, replica_groups=mesh['fibre'=64,'tm'=8] {'tm'}, dimensions={0} | all-to-all | bytes 786432 | tf_op jit(solution)/shard_map/all_to_all | solution.py:388
  62.5 0.1 convert_reduce_fusion
  62.6 7.4 %collective-permute-start.4 = (f32[192,128]{1,0:T(8,128)S(1)}, f32[192,128]{1,0:T(8,128)S(1)}, u32[]{:S(2)}, u32[]{:S(2)}) collective-permute-start(f32[192,128]{1,0:T(8,128)S(1)} %convert_reduce_fusion), channel_id=1, source_target_pairs={{0,496},{8,504},{16,0},{24,8},{32,16},{40,24},{48,32},{56,40},{64,... | collective-permute-start | bytes 294920 | tf_op jit(solution)/shard_map/ppermute | solution.py:367
  70.0 1.6 %collective-permute-done.4.row_ref = f32[192,128]{1,0:T(8,128)S(1)} collective-permute-done((f32[192,128]{1,0:T(8,128)S(1)}, f32[192,128]{1,0:T(8,128)S(1)}, u32[]{:S(2)}, u32[]{:S(2)}) %collective-permute-start.4) | collective-permute-done | bytes 98336 | tf_op jit(solution)/shard_map/ppermute | solution.py:367
  71.7 0.0 copy-done.1
  71.7 1.1 %lag_rows.1 = f32[401,1,128]{2,1,0:T(1,128)} custom-call(f32[192,128]{1,0:T(8,128)S(1)} %collective-permute-done.4.row_ref, bf16[401,576]{1,0:T(8,128)(2,1)S(1)} %copy-done.1), custom_call_target="tpu_custom_call" | custom-call | tf_op jit(solution)/shard_map/lag_rows/pallas_call | solution.py:355
Async XLA Ops:
  7.0 27.7 %collective-permute-start = (bf16[2480,128]{1,0:T(8,128)(2,1)S(1)}, bf16[2480,128]{1,0:T(8,128)(2,1)S(1)}, u32[]{:S(2)}, u32[]{:S(2)}) collective-permute-start(bf16[2480,128]{1,0:T(8,128)(2,1)S(1)} %spectra.1.b2), channel_id=1, source_target_pairs={{0,16},{8,24},{16,32},{24,40},{32,48},{40,56},{48,64},{56,72},{64,... | collective-permute-start | bytes 1904648 | tf_op jit(solution)/shard_map/ppermute | solution.py:367
  11.9 23.7 %collective-permute-start.2 = (bf16[2480,128]{1,0:T(8,128)(2,1)S(1)}, bf16[2480,128]{1,0:T(8,128)(2,1)S(1)}, u32[]{:S(2)}, u32[]{:S(2)}) collective-permute-start(bf16[2480,128]{1,0:T(8,128)(2,1)S(1)} %spectra.1.b2), channel_id=1, source_target_pairs={{0,496},{8,504},{16,0},{24,8},{32,16},{40,24},{48,32},{56,40},{64,... | collective-permute-start | bytes 1904648 | tf_op jit(solution)/shard_map/ppermute | solution.py:367
  22.7 16.6 %collective-permute-start.1 = (bf16[2480,128]{1,0:T(8,128)(2,1)S(1)}, bf16[2480,128]{1,0:T(8,128)(2,1)S(1)}, u32[]{:S(2)}, u32[]{:S(2)}) collective-permute-start(bf16[2480,128]{1,0:T(8,128)(2,1)S(1)} %spectra.1.b2), channel_id=1, source_target_pairs={{0,8},{8,0},{16,24},{24,16},{32,40},{40,32},{48,56},{56,48},{64,72... | collective-permute-start | bytes 1904648 | tf_op jit(solution)/shard_map/ppermute | solution.py:372
  25.5 15.4 %copy-start = (f32[192,2432]{1,0:T(8,128)S(1)}, f32[192,2432]{1,0:T(8,128)}, u32[]{:S(2)}) copy-start(f32[192,2432]{1,0:T(8,128)} %constant.32.clone.inner_ref) | copy-start | bytes 5603332
  35.7 36.0 %copy-start.1 = (bf16[401,576]{1,0:T(8,128)(2,1)S(1)}, bf16[401,576]{1,0:T(8,128)(2,1)}, u32[]{:S(2)}) copy-start(bf16[401,576]{1,0:T(8,128)(2,1)} %constant.33.clone.outer_ref) | copy-start | bytes 1385860
  35.7 5.3 %collective-permute-start.3 = (bf16[2480,128]{1,0:T(8,128)(2,1)S(1)}, bf16[2480,128]{1,0:T(8,128)(2,1)S(1)}, u32[]{:S(2)}, u32[]{:S(2)}) collective-permute-start(bf16[2480,128]{1,0:T(8,128)(2,1)S(1)} %broadcast_select_fusion), channel_id=1, source_target_pairs={{0,8},{8,0},{16,24},{24,16},{32,40},{40,32},{48,56},{56,48},{64,72... | collective-permute-start | bytes 1904648 | tf_op jit(solution)/shard_map/ppermute | solution.py:372
  62.6 9.1 %collective-permute-start.4 = (f32[192,128]{1,0:T(8,128)S(1)}, f32[192,128]{1,0:T(8,128)S(1)}, u32[]{:S(2)}, u32[]{:S(2)}) collective-permute-start(f32[192,128]{1,0:T(8,128)S(1)} %convert_reduce_fusion), channel_id=1, source_target_pairs={{0,496},{8,504},{16,0},{24,8},{32,16},{40,24},{48,32},{56,40},{64,... | collective-permute-start | bytes 294920 | tf_op jit(solution)/shard_map/ppermute | solution.py:367

commit v3 on v2

--- a/solution.py
+++ b/solution.py
@@ -31,7 +31,6 @@
 SRC = 24
 TAIL = 2 * SRC
 ROWS = FN + TAIL
-TABLE = FN + 2 * SRC - 1
 HALF = 96
 RANK = 2 * HALF
 STEP = 16
@@ -167,8 +166,7 @@
 
 
 def spectrum_kernel(
-    pairs_ref, count_ref, x_hbm, first_hbm, second_hbm, out_ref,
-    xs, first, second, pad, ts, zs, ss, sems,
+    x_hbm, first_hbm, second_hbm, out_ref, xs, first, second, pad, ts, zs, ss, sems
 ):
     def load(g):
         return pltpu.make_async_copy(
@@ -224,14 +222,6 @@
     for j in range(VS):
         for c in range(CHUNKS):
             ss[j * SRC + c : j * SRC + c + 1, :] = rows[j : j + 1, c * 128 : (c + 1) * 128]
-    owner = lax.axis_index("fibre")
-    lane = lax.broadcasted_iota(jnp.int32, (1, 128), 1)
-    table = jnp.where(lane == 2 * MAXP, count_ref[0], 0)
-    for slot in range(MAXP):
-        for side in range(2):
-            offset = pairs_ref[side, slot] - owner
-            table = jnp.where(lane == slot * 2 + side, offset, table)
-    ss[TABLE - FN : TABLE - FN + 1, :] = table.astype(F32)
     out_ref[FN:ROWS, :] = ss[...].astype(BF)
 
 
@@ -239,15 +229,14 @@
     return pltpu.with_memory_space_constraint(array, pltpu.HBM)
 
 
-def spectra(pair_blocks, pair_count, samples):
-    smem = pl.BlockSpec(memory_space=pltpu.SMEM)
+def spectra(samples):
     vmem = pl.BlockSpec(memory_space=pltpu.VMEM)
     hbm = pl.BlockSpec(memory_space=pltpu.HBM)
     first = jnp.asarray(first_matrix())
     second = jnp.asarray(second_matrix())
     return pl.pallas_call(
         spectrum_kernel,
-        in_specs=[smem, smem, hbm, hbm, hbm],
+        in_specs=[hbm, hbm, hbm],
         out_specs=vmem,
         out_shape=jax.ShapeDtypeStruct((ROWS, 128), BF),
         scratch_shapes=[
@@ -262,32 +251,25 @@
         ],
         compiler_params=pltpu.CompilerParams(vmem_limit_bytes=FRONT_VMEM),
         name="spectra",
-    )(
-        in_hbm(pair_blocks), pair_count, in_hbm(samples), in_hbm(first), in_hbm(second)
-    )
-
-
-def pairs_kernel(b0, b1, b2, b3, b4, inner_ref, out_ref, receiver, source, weights):
+    )(in_hbm(samples), in_hbm(first), in_hbm(second))
+
+
+def pairs_kernel(pairs_ref, count_ref, b0, b1, b2, b3, b4, inner_ref, out_ref, receiver, source, weights):
     blocks = (b0, b1, b2, b3, b4)
-    tail = b0[FN:ROWS, :].astype(F32)
-    row = tail[TABLE - FN : TABLE - FN + 1, :].astype(jnp.int32)
-    lane = lax.broadcasted_iota(jnp.int32, (1, 128), 1)
-
-    def entry(index):
-        return jnp.sum(jnp.where(lane == index, row, 0))
-
-    even = lax.rem(lax.axis_index("fibre"), 2) == 0
-
-    def place_of(offset):
-        return jnp.where(even & (lax.rem(offset, 2) == 1), REACH - offset, offset)
-
-    count = entry(2 * MAXP)
+    owner = lax.axis_index("fibre")
+    odd = lax.rem(owner, 2) == 1
+
+    def place_of(slot, side):
+        offset = pairs_ref[side, slot] - owner
+        return jnp.where(odd & (lax.rem(offset, 2) == 1), REACH - offset, offset)
+
+    count = count_ref[0]
     spot = lax.broadcasted_iota(jnp.int32, (TAIL, 128), 1)
     real_spot = lax.rem(spot, GROUP) < SLOT
 
     def one_pair(slot, carry):
-        first = place_of(entry(2 * slot))
-        second = place_of(entry(2 * slot + 1))
+        first = place_of(slot, 0)
+        second = place_of(slot, 1)
         for place, block in enumerate(blocks):
 
             @pl.when(second == place)
@@ -324,12 +306,13 @@
     lax.fori_loop(count, MAXP, one_blank, 0)
 
 
-def pair_rows(blocks):
+def pair_rows(pair_blocks, pair_count, blocks):
     _, inner = lag_factors()
+    smem = pl.BlockSpec(memory_space=pltpu.SMEM)
     vmem = pl.BlockSpec(memory_space=pltpu.VMEM)
     return pl.pallas_call(
         pairs_kernel,
-        in_specs=[vmem] * 6,
+        in_specs=[smem] * 2 + [vmem] * 6,
         out_specs=vmem,
         out_shape=jax.ShapeDtypeStruct((MAXP * VS, RANK, 128), BF),
         scratch_shapes=[
@@ -339,7 +322,7 @@
         ],
         compiler_params=pltpu.CompilerParams(vmem_limit_bytes=28 * 2**20),
         name="pair_rows",
-    )(*blocks, jnp.asarray(inner))
+    )(pair_blocks, pair_count, *blocks, jnp.asarray(inner))
 
 
 def lags_kernel(row_ref, outer_ref, out_ref):
@@ -373,21 +356,21 @@
 
 
 def gathered(own):
-    even = lax.axis_index("fibre") % 2 == 0
-    ahead = turned(own, -2)
-    behind = turned(own, 2)
-    sibling = swapped(own)
-    other = swapped(jnp.where(even, ahead, behind))
-    return [behind, sibling, own, other, ahead]
+    even = lax.rem(lax.axis_index("fibre"), 2) == 0
+    near = turned(own, -2)
+    far = turned(near, -2)
+    three = swapped(near)
+    one = swapped(jnp.where(even, far, own))
+    return [own, one, near, three, far]
 
 
 def shards(recordings, pair_blocks, pair_count):
     samples = recordings.reshape(QN, PN, 128)
-    own = spectra(pair_blocks[0].T, pair_count, samples)
-    rows = pair_rows(gathered(own))
+    own = spectra(samples)
+    rows = pair_rows(pair_blocks[0].T, pair_count, gathered(own))
     shared = lax.all_to_all(rows, "tm", 0, 0)
     row = jnp.sum(shared.astype(F32), axis=0)
-    return lag_rows(turned(row, -2))[None].transpose(0, 2, 1, 3)
+    return lag_rows(row)[None].transpose(0, 2, 1, 3)
 
 
 def solution(mesh):

time: 73.7 us -> 82.5 us (1.12)
  waiting for transfers between devices: 13.3 us -> 22.5 us
    ppermute x3 -> x2, waiting for transfers between devices: 11.7 us -> 21.5 us  [turned(): lax.ppermute(array, 'fibre', [(i, (i + by) % size) for i in range(size)])]
    ppermute x3 -> x2, starting transfers between devices: 23 us -> 21.3 us  [turned(): lax.ppermute(array, 'fibre', [(i, (i + by) % size) for i in range(size)])]
    ppermute x2, starting transfers between devices: 6.45 us -> 8.13 us  [swapped(): return lax.ppermute(array, 'fibre', [(i, i ^ 1) for i in range(size)])]
  transfers between devices with their start and end apart: 5 -> 4, of which waited for: 4 -> 3; matrix products, arithmetic and copies ran while one was open for 0% -> 0% of each run, Pallas kernels for 0% -> 0%
where the time goes in v3:
time: 82.5 us; the launch traced here: 82.2 us
  starting transfers between devices  29.5 us (36%)
  waiting for transfers between devices  22.5 us (27%)
  blocking collectives  20.5 us (25%)
  Pallas kernels  8.81 us (11%)
    ppermute x2, waiting for transfers between devices, turned(): lax.ppermute(array, 'fibre', [(i, (i + by) % size) for i in range(size)])  21.5 us
    ppermute x2, starting transfers between devices, turned(): lax.ppermute(array, 'fibre', [(i, (i + by) % size) for i in range(size)])  21.3 us
    all_to_all x1, blocking collectives, shards(): shared = lax.all_to_all(rows, 'tm', 0, 0)  20.5 us
    ppermute x2, starting transfers between devices, swapped(): return lax.ppermute(array, 'fibre', [(i, i ^ 1) for i in range(size)])  8.13 us
    pallas_call x1, Pallas kernels, spectra(): pl.pallas_call(spectrum_kernel, in_specs=[hbm, hbm, hbm], out_specs=vmem,...  5.69 us
    pallas_call x1, Pallas kernels, pair_rows(): pl.pallas_call(pairs_kernel, in_specs=[smem] * 2 + [vmem] * 6, out_specs=...  2.05 us
  transfers between devices with their start and end apart: 4, of which 3 were waited for; matrix products, arithmetic and copies ran while one was open for 0% of the time, Pallas kernels for 0%

profile of v3, /device:TPU:1, one launch (start us, length us, event | category | flops | bytes accessed | tf_op | source)
XLA Modules:
  0.0 82.2 jit_solution(16827260346225200700)
XLA Ops:
  0.0 0.0 copy-start.2
  0.0 5.7 %spectra.1.b0 = bf16[2480,128]{1,0:T(8,128)(2,1)S(1)} custom-call(f32[75,80,128]{2,1,0:T(8,128)} %bitcast.8, bf16[160,160]{1,0:T(8,128)(2,1)} %constant.22.clone.first_hbm, bf16[38,128,160]{2,1,0:T(8,128)(2,1)} %constant.23.clone.second_hbm), custom_call_target="tpu_custom_call" | custom-call | tf_op jit(solution)/shard_map/spectra/pallas_call | solution.py:237
  5.7 0.0 copy-start
  5.7 13.8 %collective-permute-start = (bf16[2480,128]{1,0:T(8,128)(2,1)S(1)}, bf16[2480,128]{1,0:T(8,128)(2,1)}, u32[]{:S(2)}, u32[]{:S(2)}) collective-permute-start(bf16[2480,128]{1,0:T(8,128)(2,1)S(1)} %spectra.1.b0), channel_id=1, source_target_pairs={{0,496},{8,504},{16,0},{24,8},{32,16},{40,24},{48,32},{56,40},{64,... | collective-permute-start | bytes 1904648 | tf_op jit(solution)/shard_map/ppermute | solution.py:350
  19.5 12.9 %collective-permute-done.b2 = bf16[2480,128]{1,0:T(8,128)(2,1)} collective-permute-done((bf16[2480,128]{1,0:T(8,128)(2,1)S(1)}, bf16[2480,128]{1,0:T(8,128)(2,1)}, u32[]{:S(2)}, u32[]{:S(2)}) %collective-permute-start) | collective-permute-done | bytes 634912 | tf_op jit(solution)/shard_map/ppermute | solution.py:350
  32.5 7.5 %collective-permute-start.1 = (bf16[2480,128]{1,0:T(8,128)(2,1)}, bf16[2480,128]{1,0:T(8,128)(2,1)S(1)}, u32[]{:S(2)}, u32[]{:S(2)}) collective-permute-start(bf16[2480,128]{1,0:T(8,128)(2,1)} %collective-permute-done.b2), channel_id=1, source_target_pairs={{0,496},{8,504},{16,0},{24,8},{32,16},{40,24},{48,32},{56,40},{64,... | collective-permute-start | bytes 1904648 | tf_op jit(solution)/shard_map/ppermute | solution.py:350
  40.0 3.7 %collective-permute-start.3 = (bf16[2480,128]{1,0:T(8,128)(2,1)}, bf16[2480,128]{1,0:T(8,128)(2,1)S(1)}, u32[]{:S(2)}, u32[]{:S(2)}) collective-permute-start(bf16[2480,128]{1,0:T(8,128)(2,1)} %collective-permute-done.b2), channel_id=1, source_target_pairs={{0,8},{8,0},{16,24},{24,16},{32,40},{40,32},{48,56},{56,48},{64,72... | collective-permute-start | bytes 1904648 | tf_op jit(solution)/shard_map/ppermute | solution.py:355
  43.8 8.6 %collective-permute-done.1.b4 = bf16[2480,128]{1,0:T(8,128)(2,1)S(1)} collective-permute-done((bf16[2480,128]{1,0:T(8,128)(2,1)}, bf16[2480,128]{1,0:T(8,128)(2,1)S(1)}, u32[]{:S(2)}, u32[]{:S(2)}) %collective-permute-start.1) | collective-permute-done | bytes 634912 | tf_op jit(solution)/shard_map/ppermute | solution.py:350
  52.3 0.1 broadcast_select_fusion
  52.4 4.4 %collective-permute-start.2 = (bf16[2480,128]{1,0:T(8,128)(2,1)S(1)}, bf16[2480,128]{1,0:T(8,128)(2,1)S(1)}, u32[]{:S(2)}, u32[]{:S(2)}) collective-permute-start(bf16[2480,128]{1,0:T(8,128)(2,1)S(1)} %broadcast_select_fusion), channel_id=1, source_target_pairs={{0,8},{8,0},{16,24},{24,16},{32,40},{40,32},{48,56},{56,48},{64,72... | collective-permute-start | bytes 1904648 | tf_op jit(solution)/shard_map/ppermute | solution.py:355
  57.5 0.0 collective-permute-done.3.b3
  57.5 1.0 %collective-permute-done.2.b1 = bf16[2480,128]{1,0:T(8,128)(2,1)S(1)} collective-permute-done((bf16[2480,128]{1,0:T(8,128)(2,1)S(1)}, bf16[2480,128]{1,0:T(8,128)(2,1)S(1)}, u32[]{:S(2)}, u32[]{:S(2)}) %collective-permute-start.2) | collective-permute-done | bytes 634912 | tf_op jit(solution)/shard_map/ppermute | solution.py:355
  58.5 0.0 copy-done.2
  58.5 0.0 copy-done
  58.5 0.0 copy-start.1
  58.5 2.0 %pair_rows.1 = bf16[8,192,128]{2,1,0:T(8,128)(2,1)S(1)} custom-call(s32[2,4]{1,0:T(2,128)S(1)} %bitcast.7, s32[1]{0:T(128)S(6)} %copy.9.count_ref, bf16[2480,128]{1,0:T(8,128)(2,1)S(1)} %spectra.1.b0, bf16[2480,128]{1,0:T(8,128)(2,1)S(1)} %collective-permute-done.2.b1, bf16[2480,128]{1,0:T(8,128)(2,1)} %collective-permute-done.b2, ...), custom_call_target="tpu_custom_call" | custom-call | tf_op jit(solution)/shard_map/pair_rows/pallas_call | solution.py:313
  60.5 20.5 %all_to_all.5 = bf16[8,192,128]{2,1,0:T(8,128)(2,1)S(1)} all-to-all(bf16[8,192,128]{2,1,0:T(8,128)(2,1)S(1)} %pair_rows.1), channel_id=1, replica_groups=mesh['fibre'=64,'tm'=8] {'tm'}, dimensions={0} | all-to-all | bytes 786432 | tf_op jit(solution)/shard_map/all_to_all | solution.py:371
  81.1 0.1 convert_reduce_fusion.row_ref
  81.1 0.0 copy-done.1
  81.1 1.1 %lag_rows.1 = f32[401,1,128]{2,1,0:T(1,128)} custom-call(f32[192,128]{1,0:T(8,128)S(1)} %convert_reduce_fusion.row_ref, bf16[401,576]{1,0:T(8,128)(2,1)S(1)} %copy-done.1), custom_call_target="tpu_custom_call" | custom-call | tf_op jit(solution)/shard_map/lag_rows/pallas_call | solution.py:338
Async XLA Ops:
  0.0 58.5 %copy-start.2 = (s32[1,4,2]{1,2,0:T(2,128)S(1)}, s32[1,4,2]{1,2,0:T(2,128)}, u32[]{:S(2)}) copy-start(s32[1,4,2]{1,2,0:T(2,128)} %param.8) | copy-start | bytes 100
  5.7 52.8 %copy-start = (f32[192,2432]{1,0:T(8,128)S(1)}, f32[192,2432]{1,0:T(8,128)}, u32[]{:S(2)}) copy-start(f32[192,2432]{1,0:T(8,128)} %constant.24.clone.inner_ref) | copy-start | bytes 5603332
  5.7 26.8 %collective-permute-start = (bf16[2480,128]{1,0:T(8,128)(2,1)S(1)}, bf16[2480,128]{1,0:T(8,128)(2,1)}, u32[]{:S(2)}, u32[]{:S(2)}) collective-permute-start(bf16[2480,128]{1,0:T(8,128)(2,1)S(1)} %spectra.1.b0), channel_id=1, source_target_pairs={{0,496},{8,504},{16,0},{24,8},{32,16},{40,24},{48,32},{56,40},{64,... | collective-permute-start | bytes 1904648 | tf_op jit(solution)/shard_map/ppermute | solution.py:350
  32.5 19.9 %collective-permute-start.1 = (bf16[2480,128]{1,0:T(8,128)(2,1)}, bf16[2480,128]{1,0:T(8,128)(2,1)S(1)}, u32[]{:S(2)}, u32[]{:S(2)}) collective-permute-start(bf16[2480,128]{1,0:T(8,128)(2,1)} %collective-permute-done.b2), channel_id=1, source_target_pairs={{0,496},{8,504},{16,0},{24,8},{32,16},{40,24},{48,32},{56,40},{64,... | collective-permute-start | bytes 1904648 | tf_op jit(solution)/shard_map/ppermute | solution.py:350
  40.0 17.4 %collective-permute-start.3 = (bf16[2480,128]{1,0:T(8,128)(2,1)}, bf16[2480,128]{1,0:T(8,128)(2,1)S(1)}, u32[]{:S(2)}, u32[]{:S(2)}) collective-permute-start(bf16[2480,128]{1,0:T(8,128)(2,1)} %collective-permute-done.b2), channel_id=1, source_target_pairs={{0,8},{8,0},{16,24},{24,16},{32,40},{40,32},{48,56},{56,48},{64,72... | collective-permute-start | bytes 1904648 | tf_op jit(solution)/shard_map/ppermute | solution.py:355
  52.4 6.1 %collective-permute-start.2 = (bf16[2480,128]{1,0:T(8,128)(2,1)S(1)}, bf16[2480,128]{1,0:T(8,128)(2,1)S(1)}, u32[]{:S(2)}, u32[]{:S(2)}) collective-permute-start(bf16[2480,128]{1,0:T(8,128)(2,1)S(1)} %broadcast_select_fusion), channel_id=1, source_target_pairs={{0,8},{8,0},{16,24},{24,16},{32,40},{40,32},{48,56},{56,48},{64,72... | collective-permute-start | bytes 1904648 | tf_op jit(solution)/shard_map/ppermute | solution.py:355
  58.5 22.6 %copy-start.1 = (bf16[401,576]{1,0:T(8,128)(2,1)S(1)}, bf16[401,576]{1,0:T(8,128)(2,1)}, u32[]{:S(2)}) copy-start(bf16[401,576]{1,0:T(8,128)(2,1)} %constant.25.clone.outer_ref) | copy-start | bytes 1385860

commit v4 on v2

--- a/solution.py
+++ b/solution.py
@@ -269,17 +269,16 @@
 
 def pairs_kernel(b0, b1, b2, b3, b4, inner_ref, out_ref, receiver, source, weights):
     blocks = (b0, b1, b2, b3, b4)
-    tail = b0[FN:ROWS, :].astype(F32)
+    even = lax.rem(lax.axis_index("fibre"), 2) == 0
+    tail = jnp.where(even, b4[FN:ROWS, :].astype(F32), b0[FN:ROWS, :].astype(F32))
     row = tail[TABLE - FN : TABLE - FN + 1, :].astype(jnp.int32)
     lane = lax.broadcasted_iota(jnp.int32, (1, 128), 1)
 
     def entry(index):
         return jnp.sum(jnp.where(lane == index, row, 0))
 
-    even = lax.rem(lax.axis_index("fibre"), 2) == 0
-
     def place_of(offset):
-        return jnp.where(even & (lax.rem(offset, 2) == 1), REACH - offset, offset)
+        return jnp.where(even, REACH - offset, offset)
 
     count = entry(2 * MAXP)
     spot = lax.broadcasted_iota(jnp.int32, (TAIL, 128), 1)
@@ -343,14 +342,14 @@
 
 
 def lags_kernel(row_ref, outer_ref, out_ref):
-    high, low = halves(row_ref[...])
-    out_ref[:, 0, :] = dot(outer_ref[...], jnp.concatenate([high, low, high], 0))
+    row = row_ref[...]
+    out_ref[:, 0, :] = dot(outer_ref[...], jnp.concatenate([row, row], 0))
 
 
 def lag_rows(row):
     outer, _ = lag_factors()
-    high, low = split(outer * (1.0 / math.sqrt(NF * 8)))
-    table = jnp.asarray(np.concatenate([high, high, low], 1))
+    high, low = split(outer)
+    table = jnp.asarray(np.concatenate([high, low], 1))
     vmem = pl.BlockSpec(memory_space=pltpu.VMEM)
     return pl.pallas_call(
         lags_kernel,
@@ -372,13 +371,19 @@
     return lax.ppermute(array, "fibre", [(i, i ^ 1) for i in range(size)])
 
 
+def parted(array, by):
+    size = lax.axis_size("fibre")
+    return lax.ppermute(
+        array, "fibre", [(i, (i - by if i % 2 == 0 else i + by) % size) for i in range(size)]
+    )
+
+
 def gathered(own):
-    even = lax.axis_index("fibre") % 2 == 0
-    ahead = turned(own, -2)
-    behind = turned(own, 2)
+    early = parted(own, 2)
+    late = parted(own, -2)
     sibling = swapped(own)
-    other = swapped(jnp.where(even, ahead, behind))
-    return [behind, sibling, own, other, ahead]
+    other = swapped(early)
+    return [early, sibling, own, other, late]
 
 
 def shards(recordings, pair_blocks, pair_count):
@@ -386,7 +391,7 @@
     own = spectra(pair_blocks[0].T, pair_count, samples)
     rows = pair_rows(gathered(own))
     shared = lax.all_to_all(rows, "tm", 0, 0)
-    row = jnp.sum(shared.astype(F32), axis=0)
+    row = (jnp.sum(shared.astype(F32), axis=0) * (1.0 / math.sqrt(NF * shared.shape[0]))).astype(BF)
     return lag_rows(turned(row, -2))[None].transpose(0, 2, 1, 3)
 
 

time: 73.7 us -> 73.3 us (level)
  waiting for transfers between devices: 13.3 us -> 5.76 us
  starting transfers between devices: 29.5 us -> 35.1 us
  Pallas kernels: 8.51 us -> 11.5 us
    ppermute x0 -> x2, starting transfers between devices: none -> 15.7 us  [parted(): lax.ppermute(array, 'fibre', [(i, (i - by if i % 2 == 0 else i + by) % si...]
    ppermute x3 -> x1, starting transfers between devices: 23 us -> 7.43 us  [turned(): lax.ppermute(array, 'fibre', [(i, (i + by) % size) for i in range(size)])]
    ppermute x3 -> x1, waiting for transfers between devices: 11.7 us -> 1.16 us  [turned(): lax.ppermute(array, 'fibre', [(i, (i + by) % size) for i in range(size)])]
    ppermute x2, starting transfers between devices: 6.45 us -> 11.9 us  [swapped(): return lax.ppermute(array, 'fibre', [(i, i ^ 1) for i in range(size)])]
    pallas_call x1, Pallas kernels: 1.08 us -> 4.03 us  [pair_rows(): pl.pallas_call(pairs_kernel, in_specs=[vmem] * 6, out_specs=vmem, out_sha...]
    ppermute x0 -> x2, waiting for transfers between devices: none -> 2.94 us  [parted(): lax.ppermute(array, 'fibre', [(i, (i - by if i % 2 == 0 else i + by) % si...]
  transfers between devices with their start and end apart: 5 -> 5, of which waited for: 4 -> 3; matrix products, arithmetic and copies ran while one was open for 0% -> 0% of each run, Pallas kernels for 0% -> 0%
where the time goes in v4:
time: 73.3 us; the launch traced here: 73 us
  starting transfers between devices  35.1 us (48%)
  blocking collectives  19.8 us (27%)
  Pallas kernels  11.5 us (16%)
  waiting for transfers between devices  5.76 us (8%)
  between operations  0.75 us (1%)
    all_to_all x1, blocking collectives, shards(): shared = lax.all_to_all(rows, 'tm', 0, 0)  19.8 us
    ppermute x2, starting transfers between devices, parted(): lax.ppermute(array, 'fibre', [(i, (i - by if i % 2 == 0 else i + by) % si...  15.7 us
    ppermute x2, starting transfers between devices, swapped(): return lax.ppermute(array, 'fibre', [(i, i ^ 1) for i in range(size)])  11.9 us
    ppermute x1, starting transfers between devices, turned(): lax.ppermute(array, 'fibre', [(i, (i + by) % size) for i in range(size)])  7.43 us
    pallas_call x1, Pallas kernels, spectra(): pl.pallas_call(spectrum_kernel, in_specs=[smem, smem, hbm, hbm, hbm], out...  6.51 us
    pallas_call x1, Pallas kernels, pair_rows(): pl.pallas_call(pairs_kernel, in_specs=[vmem] * 6, out_specs=vmem, out_sha...  4.03 us
    ppermute x2, waiting for transfers between devices, parted(): lax.ppermute(array, 'fibre', [(i, (i - by if i % 2 == 0 else i + by) % si...  2.94 us
    ppermute x2, waiting for transfers between devices, swapped(): return lax.ppermute(array, 'fibre', [(i, i ^ 1) for i in range(size)])  1.65 us
  transfers between devices with their start and end apart: 5, of which 3 were waited for; matrix products, arithmetic and copies ran while one was open for 0% of the time, Pallas kernels for 0%

profile of v4, /device:TPU:1, one launch (start us, length us, event | category | flops | bytes accessed | tf_op | source)
XLA Modules:
  0.0 73.0 jit_solution(8269447807499200365)
XLA Ops:
  0.7 0.0 copy-start
  0.7 6.5 %spectra.1.b2 = bf16[2480,128]{1,0:T(8,128)(2,1)S(1)} custom-call(s32[2,4]{1,0:T(2,128)} %bitcast.8, s32[1]{0:T(128)S(6)} %copy.9.count_ref, f32[75,80,128]{2,1,0:T(8,128)} %bitcast.7, bf16[160,160]{1,0:T(8,128)(2,1)} %constant.12.clone.first_hbm, bf16[38,128,160]{2,1,0:T(8,128)(2,1)} %constant.13.clone.second_hbm), custom_call_target="tpu_custom_call" | custom-call | tf_op jit(solution)/shard_map/spectra/pallas_call | solution.py:248
  7.2 0.0 copy-start.1
  7.2 5.0 %collective-permute-start = (bf16[2480,128]{1,0:T(8,128)(2,1)S(1)}, bf16[2480,128]{1,0:T(8,128)(2,1)S(1)}, u32[]{:S(2)}, u32[]{:S(2)}) collective-permute-start(bf16[2480,128]{1,0:T(8,128)(2,1)S(1)} %spectra.1.b2), channel_id=1, source_target_pairs={{0,496},{8,24},{16,0},{24,40},{32,16},{40,56},{48,32},{56,72},{64,... | collective-permute-start | bytes 1904648 | tf_op jit(solution)/shard_map/ppermute | solution.py:376
  12.2 10.8 %collective-permute-start.3 = (bf16[2480,128]{1,0:T(8,128)(2,1)S(1)}, bf16[2480,128]{1,0:T(8,128)(2,1)S(1)}, u32[]{:S(2)}, u32[]{:S(2)}) collective-permute-start(bf16[2480,128]{1,0:T(8,128)(2,1)S(1)} %spectra.1.b2), channel_id=1, source_target_pairs={{0,16},{8,504},{16,32},{24,8},{32,48},{40,24},{48,64},{56,40},{64,... | collective-permute-start | bytes 1904648 | tf_op jit(solution)/shard_map/ppermute | solution.py:376
  23.0 2.9 %collective-permute-start.1 = (bf16[2480,128]{1,0:T(8,128)(2,1)S(1)}, bf16[2480,128]{1,0:T(8,128)(2,1)S(1)}, u32[]{:S(2)}, u32[]{:S(2)}) collective-permute-start(bf16[2480,128]{1,0:T(8,128)(2,1)S(1)} %spectra.1.b2), channel_id=1, source_target_pairs={{0,8},{8,0},{16,24},{24,16},{32,40},{40,32},{48,56},{56,48},{64,72... | collective-permute-start | bytes 1904648 | tf_op jit(solution)/shard_map/ppermute | solution.py:371
  25.8 2.9 %collective-permute-done.b0 = bf16[2480,128]{1,0:T(8,128)(2,1)S(1)} collective-permute-done((bf16[2480,128]{1,0:T(8,128)(2,1)S(1)}, bf16[2480,128]{1,0:T(8,128)(2,1)S(1)}, u32[]{:S(2)}, u32[]{:S(2)}) %collective-permute-start) | collective-permute-done | bytes 634912 | tf_op jit(solution)/shard_map/ppermute | solution.py:376
  28.8 9.0 %collective-permute-start.2 = (bf16[2480,128]{1,0:T(8,128)(2,1)S(1)}, bf16[2480,128]{1,0:T(8,128)(2,1)S(1)}, u32[]{:S(2)}, u32[]{:S(2)}) collective-permute-start(bf16[2480,128]{1,0:T(8,128)(2,1)S(1)} %collective-permute-done.b0), channel_id=1, source_target_pairs={{0,8},{8,0},{16,24},{24,16},{32,40},{40,32},{48,56},{56,48},{64,72... | collective-permute-start | bytes 1904648 | tf_op jit(solution)/shard_map/ppermute | solution.py:371
  37.8 0.0 collective-permute-done.3.b4
  37.8 0.0 collective-permute-done.1.b1
  37.8 1.7 %collective-permute-done.2.b3 = bf16[2480,128]{1,0:T(8,128)(2,1)S(1)} collective-permute-done((bf16[2480,128]{1,0:T(8,128)(2,1)S(1)}, bf16[2480,128]{1,0:T(8,128)(2,1)S(1)}, u32[]{:S(2)}, u32[]{:S(2)}) %collective-permute-start.2) | collective-permute-done | bytes 634912 | tf_op jit(solution)/shard_map/ppermute | solution.py:371
  39.5 0.0 copy-done
  39.5 4.0 %pair_rows.1 = bf16[8,192,128]{2,1,0:T(8,128)(2,1)S(1)} custom-call(bf16[2480,128]{1,0:T(8,128)(2,1)S(1)} %collective-permute-done.b0, bf16[2480,128]{1,0:T(8,128)(2,1)S(1)} %collective-permute-done.1.b1, bf16[2480,128]{1,0:T(8,128)(2,1)S(1)} %spectra.1.b2, bf16[2480,128]{1,0:T(8,128)(2,1)S(1)} %collective-permute-done.2.b3, ...), custom_call_target="tpu_custom_call" | custom-call | tf_op jit(solution)/shard_map/pair_rows/pallas_call | solution.py:329
  43.5 19.8 %all_to_all.5 = bf16[8,192,128]{2,1,0:T(8,128)(2,1)S(1)} all-to-all(bf16[8,192,128]{2,1,0:T(8,128)(2,1)S(1)} %pair_rows.1), channel_id=1, replica_groups=mesh['fibre'=64,'tm'=8] {'tm'}, dimensions={0} | all-to-all | bytes 786432 | tf_op jit(solution)/shard_map/all_to_all | solution.py:393
  63.3 0.1 convert_reduce_fusion
  63.4 7.4 %collective-permute-start.4 = (bf16[192,128]{1,0:T(8,128)(2,1)S(1)}, bf16[192,128]{1,0:T(8,128)(2,1)S(1)}, u32[]{:S(2)}, u32[]{:S(2)}) collective-permute-start(bf16[192,128]{1,0:T(8,128)(2,1)S(1)} %multiply_convert_fusion), channel_id=1, source_target_pairs={{0,496},{8,504},{16,0},{24,8},{32,16},{40,24},{48,32},{56,40},{64,... | collective-permute-start | bytes 147464 | tf_op jit(solution)/shard_map/ppermute | solution.py:366
  70.8 1.2 %collective-permute-done.4.row_ref = bf16[192,128]{1,0:T(8,128)(2,1)S(1)} collective-permute-done((bf16[192,128]{1,0:T(8,128)(2,1)S(1)}, bf16[192,128]{1,0:T(8,128)(2,1)S(1)}, u32[]{:S(2)}, u32[]{:S(2)}) %collective-permute-start.4) | collective-permute-done | bytes 49184 | tf_op jit(solution)/shard_map/ppermute | solution.py:366
  72.0 0.0 copy-done.1
  72.0 1.0 %lag_rows.1 = f32[401,1,128]{2,1,0:T(1,128)} custom-call(bf16[192,128]{1,0:T(8,128)(2,1)S(1)} %collective-permute-done.4.row_ref, bf16[401,384]{1,0:T(8,128)(2,1)S(1)} %copy-done.1), custom_call_target="tpu_custom_call" | custom-call | tf_op jit(solution)/shard_map/lag_rows/pallas_call | solution.py:354
  (1 shorter events, 0.0 us)
Async XLA Ops:
  0.7 38.8 %copy-start = (f32[192,2432]{1,0:T(8,128)S(1)}, f32[192,2432]{1,0:T(8,128)}, u32[]{:S(2)}) copy-start(f32[192,2432]{1,0:T(8,128)} %constant.14.clone.inner_ref) | copy-start | bytes 5603332
  7.2 64.8 %copy-start.1 = (bf16[401,384]{1,0:T(8,128)(2,1)S(1)}, bf16[401,384]{1,0:T(8,128)(2,1)}, u32[]{:S(2)}) copy-start(bf16[401,384]{1,0:T(8,128)(2,1)} %constant.15.clone.outer_ref) | copy-start | bytes 923908
  7.2 21.6 %collective-permute-start = (bf16[2480,128]{1,0:T(8,128)(2,1)S(1)}, bf16[2480,128]{1,0:T(8,128)(2,1)S(1)}, u32[]{:S(2)}, u32[]{:S(2)}) collective-permute-start(bf16[2480,128]{1,0:T(8,128)(2,1)S(1)} %spectra.1.b2), channel_id=1, source_target_pairs={{0,496},{8,24},{16,0},{24,40},{32,16},{40,56},{48,32},{56,72},{64,... | collective-permute-start | bytes 1904648 | tf_op jit(solution)/shard_map/ppermute | solution.py:376
  12.2 25.6 %collective-permute-start.3 = (bf16[2480,128]{1,0:T(8,128)(2,1)S(1)}, bf16[2480,128]{1,0:T(8,128)(2,1)S(1)}, u32[]{:S(2)}, u32[]{:S(2)}) collective-permute-start(bf16[2480,128]{1,0:T(8,128)(2,1)S(1)} %spectra.1.b2), channel_id=1, source_target_pairs={{0,16},{8,504},{16,32},{24,8},{32,48},{40,24},{48,64},{56,40},{64,... | collective-permute-start | bytes 1904648 | tf_op jit(solution)/shard_map/ppermute | solution.py:376
  23.0 14.8 %collective-permute-start.1 = (bf16[2480,128]{1,0:T(8,128)(2,1)S(1)}, bf16[2480,128]{1,0:T(8,128)(2,1)S(1)}, u32[]{:S(2)}, u32[]{:S(2)}) collective-permute-start(bf16[2480,128]{1,0:T(8,128)(2,1)S(1)} %spectra.1.b2), channel_id=1, source_target_pairs={{0,8},{8,0},{16,24},{24,16},{32,40},{40,32},{48,56},{56,48},{64,72... | collective-permute-start | bytes 1904648 | tf_op jit(solution)/shard_map/ppermute | solution.py:371
  28.8 10.7 %collective-permute-start.2 = (bf16[2480,128]{1,0:T(8,128)(2,1)S(1)}, bf16[2480,128]{1,0:T(8,128)(2,1)S(1)}, u32[]{:S(2)}, u32[]{:S(2)}) collective-permute-start(bf16[2480,128]{1,0:T(8,128)(2,1)S(1)} %collective-permute-done.b0), channel_id=1, source_target_pairs={{0,8},{8,0},{16,24},{24,16},{32,40},{40,32},{48,56},{56,48},{64,72... | collective-permute-start | bytes 1904648 | tf_op jit(solution)/shard_map/ppermute | solution.py:371
  63.4 8.6 %collective-permute-start.4 = (bf16[192,128]{1,0:T(8,128)(2,1)S(1)}, bf16[192,128]{1,0:T(8,128)(2,1)S(1)}, u32[]{:S(2)}, u32[]{:S(2)}) collective-permute-start(bf16[192,128]{1,0:T(8,128)(2,1)S(1)} %multiply_convert_fusion), channel_id=1, source_target_pairs={{0,496},{8,504},{16,0},{24,8},{32,16},{40,24},{48,32},{56,40},{64,... | collective-permute-start | bytes 147464 | tf_op jit(solution)/shard_map/ppermute | solution.py:366

commit v5 on v4

--- a/solution.py
+++ b/solution.py
@@ -24,6 +24,7 @@
 KN = 38
 KPAD = 40
 QPAD = 80
+WIDE = 2 * PN + 8
 SLOT = 32
 GROUP = 2 * SLOT
 FN = KN * GROUP
@@ -34,7 +35,7 @@
 TABLE = FN + 2 * SRC - 1
 HALF = 96
 RANK = 2 * HALF
-STEP = 16
+STEP = 40
 STEPS = PN // STEP
 UNROLL = 19
 FRONT_VMEM = 28 * 2**20
@@ -167,8 +168,8 @@
 
 
 def spectrum_kernel(
-    pairs_ref, count_ref, x_hbm, first_hbm, second_hbm, out_ref,
-    xs, first, second, pad, ts, zs, ss, sems,
+    pairs_hbm, count_ref, x_hbm, first_hbm, second_hbm, out_ref,
+    pairs_ref, xs, first, second, pad, ts, zs, ss, sems,
 ):
     def load(g):
         return pltpu.make_async_copy(
@@ -181,6 +182,8 @@
     for g in range(STEPS):
         load(g).start()
     second_copy.start()
+    pairs_copy = pltpu.make_async_copy(pairs_hbm, pairs_ref, sems.at[STEPS + 2])
+    pairs_copy.start()
     pad[72:80, :] = jnp.zeros((8, STEP * 128), F32)
 
     def sections(g, carry):
@@ -195,8 +198,8 @@
             for side in range(2):
                 p = g * STEP + pair * 2 + side
                 part = section[:, side * 128 : (side + 1) * 128]
-                ts[pl.ds(p, KPAD, stride=2 * PN), :] = part[:KPAD]
-                ts[pl.ds(PN + p, KPAD, stride=2 * PN), :] = part[KPAD:]
+                ts[pl.ds(p, KPAD, stride=WIDE), :] = part[:KPAD]
+                ts[pl.ds(PN + p, KPAD, stride=WIDE), :] = part[KPAD:]
         return carry
 
     first_copy.wait()
@@ -204,7 +207,7 @@
     second_copy.wait()
 
     def residue(k, power):
-        high, low = halves(ts[pl.ds(pl.multiple_of(k * 2 * PN, 2 * PN), 2 * PN), :])
+        high, low = halves(ts[pl.ds(pl.multiple_of(k * WIDE, 8), 2 * PN), :])
         product = dot(second[k], jnp.concatenate([high, low], 1))
         value = product[:GROUP, :128] + (product[:GROUP, 128:] + product[GROUP:, :128])
         zs[pl.ds(pl.multiple_of(k * GROUP, GROUP), GROUP), :] = value
@@ -224,6 +227,7 @@
     for j in range(VS):
         for c in range(CHUNKS):
             ss[j * SRC + c : j * SRC + c + 1, :] = rows[j : j + 1, c * 128 : (c + 1) * 128]
+    pairs_copy.wait()
     owner = lax.axis_index("fibre")
     lane = lax.broadcasted_iota(jnp.int32, (1, 128), 1)
     table = jnp.where(lane == 2 * MAXP, count_ref[0], 0)
@@ -240,25 +244,25 @@
 
 
 def spectra(pair_blocks, pair_count, samples):
-    smem = pl.BlockSpec(memory_space=pltpu.SMEM)
     vmem = pl.BlockSpec(memory_space=pltpu.VMEM)
     hbm = pl.BlockSpec(memory_space=pltpu.HBM)
     first = jnp.asarray(first_matrix())
     second = jnp.asarray(second_matrix())
     return pl.pallas_call(
         spectrum_kernel,
-        in_specs=[smem, smem, hbm, hbm, hbm],
+        in_specs=[hbm, pl.BlockSpec(memory_space=pltpu.SMEM), hbm, hbm, hbm],
         out_specs=vmem,
         out_shape=jax.ShapeDtypeStruct((ROWS, 128), BF),
         scratch_shapes=[
+            pltpu.SMEM(pair_blocks.shape, jnp.int32),
             pltpu.VMEM((STEPS, QN, STEP, 128), F32),
             pltpu.VMEM(first.shape, BF),
             pltpu.VMEM(second.shape, BF),
             pltpu.VMEM((QPAD, STEP * 128), F32),
-            pltpu.VMEM((KPAD * 2 * PN, 128), F32),
+            pltpu.VMEM((KPAD * WIDE, 128), F32),
             pltpu.VMEM((FN, 128), F32),
             pltpu.VMEM((TAIL, 128), F32),
-            pltpu.SemaphoreType.DMA((STEPS + 2,)),
+            pltpu.SemaphoreType.DMA((STEPS + 3,)),
         ],
         compiler_params=pltpu.CompilerParams(vmem_limit_bytes=FRONT_VMEM),
         name="spectra",

time: 73.3 us -> 69 us (0.941)
  the two profiles are of different devices: /device:TPU:1 before, /device:TPU:8 now
where the time goes in v5:
time: 69 us; the launch traced here: 68.9 us
  starting transfers between devices  26.7 us (39%)
  blocking collectives  20.9 us (30%)
  waiting for transfers between devices  13.8 us (20%)
  Pallas kernels  6.6 us (10%)
  between operations  0.75 us (1%)
    all_to_all x1, blocking collectives, shards(): shared = lax.all_to_all(rows, 'tm', 0, 0)  20.9 us
    ppermute x2, starting transfers between devices, parted(): lax.ppermute(array, 'fibre', [(i, (i - by if i % 2 == 0 else i + by) % si...  15.2 us
    ppermute x2, waiting for transfers between devices, parted(): lax.ppermute(array, 'fibre', [(i, (i - by if i % 2 == 0 else i + by) % si...  10 us
    ppermute x1, starting transfers between devices, turned(): lax.ppermute(array, 'fibre', [(i, (i + by) % size) for i in range(size)])  7.71 us
    pallas_call x1, Pallas kernels, spectra(): pl.pallas_call(spectrum_kernel, in_specs=[hbm, pl.BlockSpec(memory_space=...  4.46 us
    ppermute x2, starting transfers between devices, swapped(): return lax.ppermute(array, 'fibre', [(i, i ^ 1) for i in range(size)])  3.83 us
    ppermute x2, waiting for transfers between devices, swapped(): return lax.ppermute(array, 'fibre', [(i, i ^ 1) for i in range(size)])  2.02 us
    ppermute x1, waiting for transfers between devices, turned(): lax.ppermute(array, 'fibre', [(i, (i + by) % size) for i in range(size)])  1.73 us
  transfers between devices with their start and end apart: 5, of which 3 were waited for; matrix products, arithmetic and copies ran while one was open for 0% of the time, Pallas kernels for 0%

profile of v5, /device:TPU:8, one launch (start us, length us, event | category | flops | bytes accessed | tf_op | source)
XLA Modules:
  0.0 68.9 jit_solution(15549453299282172752)
XLA Ops:
  0.7 0.0 copy-start
  0.7 4.5 %spectra.1.b2 = bf16[2480,128]{1,0:T(8,128)(2,1)S(1)} custom-call(s32[2,4]{1,0:T(2,128)} %bitcast.8, s32[1]{0:T(128)S(6)} %copy.9.count_ref, f32[75,80,128]{2,1,0:T(8,128)} %bitcast.7, bf16[160,160]{1,0:T(8,128)(2,1)} %constant.12.clone.first_hbm, bf16[38,128,160]{2,1,0:T(8,128)(2,1)} %constant.13.clone.second_hbm), custom_call_target="tpu_custom_call" | custom-call | tf_op jit(solution)/shard_map/spectra/pallas_call | solution.py:251
  5.1 0.0 copy-start.1
  5.1 13.3 %collective-permute-start = (bf16[2480,128]{1,0:T(8,128)(2,1)S(1)}, bf16[2480,128]{1,0:T(8,128)(2,1)S(1)}, u32[]{:S(2)}, u32[]{:S(2)}) collective-permute-start(bf16[2480,128]{1,0:T(8,128)(2,1)S(1)} %spectra.1.b2), channel_id=1, source_target_pairs={{0,496},{8,24},{16,0},{24,40},{32,16},{40,56},{48,32},{56,72},{64,... | collective-permute-start | bytes 1904648 | tf_op jit(solution)/shard_map/ppermute | solution.py:380
  18.4 1.9 %collective-permute-start.3 = (bf16[2480,128]{1,0:T(8,128)(2,1)S(1)}, bf16[2480,128]{1,0:T(8,128)(2,1)S(1)}, u32[]{:S(2)}, u32[]{:S(2)}) collective-permute-start(bf16[2480,128]{1,0:T(8,128)(2,1)S(1)} %spectra.1.b2), channel_id=1, source_target_pairs={{0,16},{8,504},{16,32},{24,8},{32,48},{40,24},{48,64},{56,40},{64,... | collective-permute-start | bytes 1904648 | tf_op jit(solution)/shard_map/ppermute | solution.py:380
  20.4 1.9 %collective-permute-start.1 = (bf16[2480,128]{1,0:T(8,128)(2,1)S(1)}, bf16[2480,128]{1,0:T(8,128)(2,1)S(1)}, u32[]{:S(2)}, u32[]{:S(2)}) collective-permute-start(bf16[2480,128]{1,0:T(8,128)(2,1)S(1)} %spectra.1.b2), channel_id=1, source_target_pairs={{0,8},{8,0},{16,24},{24,16},{32,40},{40,32},{48,56},{56,48},{64,72... | collective-permute-start | bytes 1904648 | tf_op jit(solution)/shard_map/ppermute | solution.py:375
  22.3 10.0 %collective-permute-done.b0 = bf16[2480,128]{1,0:T(8,128)(2,1)S(1)} collective-permute-done((bf16[2480,128]{1,0:T(8,128)(2,1)S(1)}, bf16[2480,128]{1,0:T(8,128)(2,1)S(1)}, u32[]{:S(2)}, u32[]{:S(2)}) %collective-permute-start) | collective-permute-done | bytes 634912 | tf_op jit(solution)/shard_map/ppermute | solution.py:380
  32.3 1.9 %collective-permute-start.2 = (bf16[2480,128]{1,0:T(8,128)(2,1)S(1)}, bf16[2480,128]{1,0:T(8,128)(2,1)S(1)}, u32[]{:S(2)}, u32[]{:S(2)}) collective-permute-start(bf16[2480,128]{1,0:T(8,128)(2,1)S(1)} %collective-permute-done.b0), channel_id=1, source_target_pairs={{0,8},{8,0},{16,24},{24,16},{32,40},{40,32},{48,56},{56,48},{64,72... | collective-permute-start | bytes 1904648 | tf_op jit(solution)/shard_map/ppermute | solution.py:375
  34.2 0.0 collective-permute-done.3.b4
  34.2 0.0 collective-permute-done.1.b1
  34.3 2.0 %collective-permute-done.2.b3 = bf16[2480,128]{1,0:T(8,128)(2,1)S(1)} collective-permute-done((bf16[2480,128]{1,0:T(8,128)(2,1)S(1)}, bf16[2480,128]{1,0:T(8,128)(2,1)S(1)}, u32[]{:S(2)}, u32[]{:S(2)}) %collective-permute-start.2) | collective-permute-done | bytes 634912 | tf_op jit(solution)/shard_map/ppermute | solution.py:375
  36.3 0.0 copy-done
  36.3 1.1 %pair_rows.1 = bf16[8,192,128]{2,1,0:T(8,128)(2,1)S(1)} custom-call(bf16[2480,128]{1,0:T(8,128)(2,1)S(1)} %collective-permute-done.b0, bf16[2480,128]{1,0:T(8,128)(2,1)S(1)} %collective-permute-done.1.b1, bf16[2480,128]{1,0:T(8,128)(2,1)S(1)} %spectra.1.b2, bf16[2480,128]{1,0:T(8,128)(2,1)S(1)} %collective-permute-done.2.b3, ...), custom_call_target="tpu_custom_call" | custom-call | tf_op jit(solution)/shard_map/pair_rows/pallas_call | solution.py:333
  37.4 20.9 %all_to_all.5 = bf16[8,192,128]{2,1,0:T(8,128)(2,1)S(1)} all-to-all(bf16[8,192,128]{2,1,0:T(8,128)(2,1)S(1)} %pair_rows.1), channel_id=1, replica_groups=mesh['fibre'=64,'tm'=8] {'tm'}, dimensions={0} | all-to-all | bytes 786432 | tf_op jit(solution)/shard_map/all_to_all | solution.py:397
  58.3 0.1 convert_reduce_fusion
  58.4 7.7 %collective-permute-start.4 = (bf16[192,128]{1,0:T(8,128)(2,1)S(1)}, bf16[192,128]{1,0:T(8,128)(2,1)S(1)}, u32[]{:S(2)}, u32[]{:S(2)}) collective-permute-start(bf16[192,128]{1,0:T(8,128)(2,1)S(1)} %multiply_convert_fusion), channel_id=1, source_target_pairs={{0,496},{8,504},{16,0},{24,8},{32,16},{40,24},{48,32},{56,40},{64,... | collective-permute-start | bytes 147464 | tf_op jit(solution)/shard_map/ppermute | solution.py:370
  66.1 1.7 %collective-permute-done.4.row_ref = bf16[192,128]{1,0:T(8,128)(2,1)S(1)} collective-permute-done((bf16[192,128]{1,0:T(8,128)(2,1)S(1)}, bf16[192,128]{1,0:T(8,128)(2,1)S(1)}, u32[]{:S(2)}, u32[]{:S(2)}) %collective-permute-start.4) | collective-permute-done | bytes 49184 | tf_op jit(solution)/shard_map/ppermute | solution.py:370
  67.9 0.0 copy-done.1
  67.9 1.0 %lag_rows.1 = f32[401,1,128]{2,1,0:T(1,128)} custom-call(bf16[192,128]{1,0:T(8,128)(2,1)S(1)} %collective-permute-done.4.row_ref, bf16[401,384]{1,0:T(8,128)(2,1)S(1)} %copy-done.1), custom_call_target="tpu_custom_call" | custom-call | tf_op jit(solution)/shard_map/lag_rows/pallas_call | solution.py:358
  (1 shorter events, 0.0 us)
Async XLA Ops:
  0.7 35.6 %copy-start = (f32[192,2432]{1,0:T(8,128)S(1)}, f32[192,2432]{1,0:T(8,128)}, u32[]{:S(2)}) copy-start(f32[192,2432]{1,0:T(8,128)} %constant.14.clone.inner_ref) | copy-start | bytes 5603332
  5.1 62.7 %copy-start.1 = (bf16[401,384]{1,0:T(8,128)(2,1)S(1)}, bf16[401,384]{1,0:T(8,128)(2,1)}, u32[]{:S(2)}) copy-start(bf16[401,384]{1,0:T(8,128)(2,1)} %constant.15.clone.outer_ref) | copy-start | bytes 923908
  5.1 27.2 %collective-permute-start = (bf16[2480,128]{1,0:T(8,128)(2,1)S(1)}, bf16[2480,128]{1,0:T(8,128)(2,1)S(1)}, u32[]{:S(2)}, u32[]{:S(2)}) collective-permute-start(bf16[2480,128]{1,0:T(8,128)(2,1)S(1)} %spectra.1.b2), channel_id=1, source_target_pairs={{0,496},{8,24},{16,0},{24,40},{32,16},{40,56},{48,32},{56,72},{64,... | collective-permute-start | bytes 1904648 | tf_op jit(solution)/shard_map/ppermute | solution.py:380
  18.4 15.8 %collective-permute-start.3 = (bf16[2480,128]{1,0:T(8,128)(2,1)S(1)}, bf16[2480,128]{1,0:T(8,128)(2,1)S(1)}, u32[]{:S(2)}, u32[]{:S(2)}) collective-permute-start(bf16[2480,128]{1,0:T(8,128)(2,1)S(1)} %spectra.1.b2), channel_id=1, source_target_pairs={{0,16},{8,504},{16,32},{24,8},{32,48},{40,24},{48,64},{56,40},{64,... | collective-permute-start | bytes 1904648 | tf_op jit(solution)/shard_map/ppermute | solution.py:380
  20.4 13.9 %collective-permute-start.1 = (bf16[2480,128]{1,0:T(8,128)(2,1)S(1)}, bf16[2480,128]{1,0:T(8,128)(2,1)S(1)}, u32[]{:S(2)}, u32[]{:S(2)}) collective-permute-start(bf16[2480,128]{1,0:T(8,128)(2,1)S(1)} %spectra.1.b2), channel_id=1, source_target_pairs={{0,8},{8,0},{16,24},{24,16},{32,40},{40,32},{48,56},{56,48},{64,72... | collective-permute-start | bytes 1904648 | tf_op jit(solution)/shard_map/ppermute | solution.py:375
  32.3 4.0 %collective-permute-start.2 = (bf16[2480,128]{1,0:T(8,128)(2,1)S(1)}, bf16[2480,128]{1,0:T(8,128)(2,1)S(1)}, u32[]{:S(2)}, u32[]{:S(2)}) collective-permute-start(bf16[2480,128]{1,0:T(8,128)(2,1)S(1)} %collective-permute-done.b0), channel_id=1, source_target_pairs={{0,8},{8,0},{16,24},{24,16},{32,40},{40,32},{48,56},{56,48},{64,72... | collective-permute-start | bytes 1904648 | tf_op jit(solution)/shard_map/ppermute | solution.py:375
  58.4 9.4 %collective-permute-start.4 = (bf16[192,128]{1,0:T(8,128)(2,1)S(1)}, bf16[192,128]{1,0:T(8,128)(2,1)S(1)}, u32[]{:S(2)}, u32[]{:S(2)}) collective-permute-start(bf16[192,128]{1,0:T(8,128)(2,1)S(1)} %multiply_convert_fusion), channel_id=1, source_target_pairs={{0,496},{8,504},{16,0},{24,8},{32,16},{40,24},{48,32},{56,40},{64,... | collective-permute-start | bytes 147464 | tf_op jit(solution)/shard_map/ppermute | solution.py:370

commit v6 on v5

--- a/solution.py
+++ b/solution.py
@@ -28,11 +28,11 @@
 SLOT = 32
 GROUP = 2 * SLOT
 FN = KN * GROUP
-CHUNKS = FN // 128
-SRC = 24
-TAIL = 2 * SRC
+BINS = KN * SLOT
+CHUNKS = -(-BINS // 128)
+TAIL = 48
 ROWS = FN + TAIL
-TABLE = FN + 2 * SRC - 1
+TABLE = ROWS - 1
 HALF = 96
 RANK = 2 * HALF
 STEP = 40
@@ -139,22 +139,18 @@
     odd_table = sine(lag[1:] * band)
     even = basis(even_table)
     odd = basis(odd_table)
-    inner = np.zeros((RANK, KN, 2, SLOT))
+    inner = np.zeros((2, HALF, KN, SLOT))
     place = np.maximum(bins - F0, 0)
     for i in range(HALF):
-        row = (even[i][:, None] * even_table).sum(0)[place] * live
-        inner[i, :, 0] = row
-        inner[i, :, 1] = row
-        row = (odd[i][:, None] * odd_table).sum(0)[place] * live
-        inner[HALF + i, :, 0] = -row
-        inner[HALF + i, :, 1] = row
+        inner[0, i] = (even[i][:, None] * even_table).sum(0)[place] * live
+        inner[1, i] = (odd[i][:, None] * odd_table).sum(0)[place] * live
     outer = np.zeros((LAGS, RANK))
     for i in range(HALF):
         outer[MAXLAG:, i] = even[i]
         outer[MAXLAG::-1, i] = even[i]
         outer[MAXLAG + 1 :, HALF + i] = -odd[i]
         outer[MAXLAG - 1 :: -1, HALF + i] = odd[i]
-    return outer, inner.reshape(RANK, FN).astype(np.float32)
+    return outer, inner.reshape(RANK, BINS).astype(np.float32)
 
 
 def halves(value):
@@ -210,7 +206,9 @@
         high, low = halves(ts[pl.ds(pl.multiple_of(k * WIDE, 8), 2 * PN), :])
         product = dot(second[k], jnp.concatenate([high, low], 1))
         value = product[:GROUP, :128] + (product[:GROUP, 128:] + product[GROUP:, :128])
-        zs[pl.ds(pl.multiple_of(k * GROUP, GROUP), GROUP), :] = value
+        at = pl.multiple_of(k * SLOT, SLOT)
+        zs[pl.ds(at, SLOT), :] = value[:SLOT]
+        zs[pl.ds(BINS + at, SLOT), :] = value[SLOT:]
         return power + jnp.sum((value * value).reshape(GROUP // 8, 8, 128), axis=0)
 
     power = lax.fori_loop(0, KN, residue, jnp.zeros((8, 128), F32), unroll=UNROLL)
@@ -220,13 +218,19 @@
     lane = lax.broadcasted_iota(jnp.int32, (8, 128), 1)
     sub = lax.broadcasted_iota(jnp.int32, (8, 128), 0)
     pick = jnp.where(lane == sub * (128 // VS), 1.0, 0.0).astype(BF)
-    rows = lax.dot_general(
-        pick, out_ref[0:FN, :], (((1,), (1,)), ((), ())), preferred_element_type=F32
-    )
     ss[...] = jnp.zeros_like(ss)
-    for j in range(VS):
-        for c in range(CHUNKS):
-            ss[j * SRC + c : j * SRC + c + 1, :] = rows[j : j + 1, c * 128 : (c + 1) * 128]
+    for part in range(2):
+        rows = lax.dot_general(
+            pick,
+            out_ref[part * BINS : (part + 1) * BINS, :],
+            (((1,), (1,)), ((), ())),
+            preferred_element_type=F32,
+        )
+        for j in range(VS):
+            for c in range(CHUNKS):
+                at = (j * 2 + part) * CHUNKS + c
+                wide = min(128, BINS - c * 128)
+                ss[at : at + 1, 0:wide] = rows[j : j + 1, c * 128 : c * 128 + wide]
     pairs_copy.wait()
     owner = lax.axis_index("fibre")
     lane = lax.broadcasted_iota(jnp.int32, (1, 128), 1)
@@ -271,51 +275,52 @@
     )
 
 
-def pairs_kernel(b0, b1, b2, b3, b4, inner_ref, out_ref, receiver, source, weights):
+def pairs_kernel(
+    b0, b1, b2, b3, b4, inner_ref, out_ref, entries, receiver, source, weights
+):
     blocks = (b0, b1, b2, b3, b4)
     even = lax.rem(lax.axis_index("fibre"), 2) == 0
     tail = jnp.where(even, b4[FN:ROWS, :].astype(F32), b0[FN:ROWS, :].astype(F32))
     row = tail[TABLE - FN : TABLE - FN + 1, :].astype(jnp.int32)
     lane = lax.broadcasted_iota(jnp.int32, (1, 128), 1)
-
-    def entry(index):
-        return jnp.sum(jnp.where(lane == index, row, 0))
+    for index in range(2 * MAXP + 1):
+        entries[index] = jnp.sum(jnp.where(lane == index, row, 0))
 
     def place_of(offset):
         return jnp.where(even, REACH - offset, offset)
 
-    count = entry(2 * MAXP)
-    spot = lax.broadcasted_iota(jnp.int32, (TAIL, 128), 1)
-    real_spot = lax.rem(spot, GROUP) < SLOT
+    count = entries[2 * MAXP]
 
     def one_pair(slot, carry):
-        first = place_of(entry(2 * slot))
-        second = place_of(entry(2 * slot + 1))
+        first = place_of(entries[2 * slot])
+        second = place_of(entries[2 * slot + 1])
         for place, block in enumerate(blocks):
 
             @pl.when(second == place)
             def _():
-                receiver[...] = block[0:FN, :]
+                receiver[:, 0:128] = block[0:BINS, :]
+                receiver[:, 128:256] = block[BINS:FN, :]
 
             @pl.when(first == place)
             def _():
                 source[...] = block[FN:ROWS, :].astype(F32)
 
-        straight = source[...]
-        crossed = jnp.where(
-            real_spot, pltpu.roll(straight, 128 - SLOT, 1), pltpu.roll(straight, SLOT, 1)
-        )
+        for c in range(CHUNKS):
+            wide = min(128, BINS - c * 128)
+            here = slice(c * 128, c * 128 + wide)
+            table = inner_ref[:, here]
+            for part in range(2 * VS):
+                at = part * CHUNKS + c
+                scaled = table * source[at : at + 1, 0:wide]
+                weights[part * RANK : (part + 1) * RANK, here] = scaled.astype(BF)
+        product = dot(weights[...], receiver[...])
         for j in range(VS):
-            for c in range(CHUNKS):
-                at = j * SRC + c
-                here = pl.ds(c * 128, 128)
-                even = inner_ref[0:HALF, here] * straight[at : at + 1, :]
-                odd = inner_ref[HALF:RANK, here] * crossed[at : at + 1, :]
-                weights[j * RANK : j * RANK + HALF, here] = even.astype(BF)
-                weights[j * RANK + HALF : (j + 1) * RANK, here] = odd.astype(BF)
-        result = dot(weights[...], receiver[...]).astype(BF)
-        for j in range(VS):
-            out_ref[slot * VS + j] = result[j * RANK : (j + 1) * RANK]
+            real = product[(2 * j) * RANK : (2 * j + 1) * RANK]
+            imag = product[(2 * j + 1) * RANK : (2 * j + 2) * RANK]
+            same = real[:HALF, :128] + imag[:HALF, 128:]
+            turn = real[HALF:, 128:] - imag[HALF:, :128]
+            out_ref[slot * VS + j, 0:HALF, :] = same.astype(BF)
+            out_ref[slot * VS + j, HALF:RANK, :] = turn.astype(BF)
         return carry
 
     def one_blank(slot, carry):
@@ -336,9 +341,10 @@
         out_specs=vmem,
         out_shape=jax.ShapeDtypeStruct((MAXP * VS, RANK, 128), BF),
         scratch_shapes=[
-            pltpu.VMEM((FN, 128), BF),
+            pltpu.SMEM((2 * MAXP + 1,), jnp.int32),
+            pltpu.VMEM((BINS, 256), BF),
             pltpu.VMEM((TAIL, 128), F32),
-            pltpu.VMEM((VS * RANK, FN), BF),
+            pltpu.VMEM((2 * VS * RANK, BINS), BF),
         ],
         compiler_params=pltpu.CompilerParams(vmem_limit_bytes=28 * 2**20),
         name="pair_rows",

time: 69 us -> 69 us (level)
  the two profiles are of different devices: /device:TPU:8 before, /device:TPU:1 now
where the time goes in v6:
time: 69 us; the launch traced here: 68.7 us
  starting transfers between devices  35.1 us (51%)
  blocking collectives  20.5 us (30%)
  Pallas kernels  6.5 us (9%)
  waiting for transfers between devices  5.75 us (8%)
  between operations  0.75 us (1%)
    all_to_all x1, blocking collectives, shards(): shared = lax.all_to_all(rows, 'tm', 0, 0)  20.5 us
    ppermute x2, starting transfers between devices, parted(): lax.ppermute(array, 'fibre', [(i, (i - by if i % 2 == 0 else i + by) % si...  15.8 us
    ppermute x2, starting transfers between devices, swapped(): return lax.ppermute(array, 'fibre', [(i, i ^ 1) for i in range(size)])  11.9 us
    ppermute x1, starting transfers between devices, turned(): lax.ppermute(array, 'fibre', [(i, (i + by) % size) for i in range(size)])  7.43 us
    pallas_call x1, Pallas kernels, spectra(): pl.pallas_call(spectrum_kernel, in_specs=[hbm, pl.BlockSpec(memory_space=...  4.43 us
    ppermute x2, waiting for transfers between devices, parted(): lax.ppermute(array, 'fibre', [(i, (i - by if i % 2 == 0 else i + by) % si...  2.94 us
    ppermute x2, waiting for transfers between devices, swapped(): return lax.ppermute(array, 'fibre', [(i, i ^ 1) for i in range(size)])  1.65 us
  transfers between devices with their start and end apart: 5, of which 3 were waited for; matrix products, arithmetic and copies ran while one was open for 0% of the time, Pallas kernels for 0%

profile of v6, /device:TPU:1, one launch (start us, length us, event | category | flops | bytes accessed | tf_op | source)
XLA Modules:
  0.0 68.7 jit_solution(3914061881705620579)
XLA Ops:
  0.7 0.0 copy-start
  0.7 4.4 %spectra.1.b2 = bf16[2480,128]{1,0:T(8,128)(2,1)S(1)} custom-call(s32[2,4]{1,0:T(2,128)} %bitcast.8, s32[1]{0:T(128)S(6)} %copy.9.count_ref, f32[75,80,128]{2,1,0:T(8,128)} %bitcast.7, bf16[160,160]{1,0:T(8,128)(2,1)} %constant.12.clone.first_hbm, bf16[38,128,160]{2,1,0:T(8,128)(2,1)} %constant.13.clone.second_hbm), custom_call_target="tpu_custom_call" | custom-call | tf_op jit(solution)/shard_map/spectra/pallas_call | solution.py:255
  5.1 0.0 copy-start.1
  5.1 5.0 %collective-permute-start = (bf16[2480,128]{1,0:T(8,128)(2,1)S(1)}, bf16[2480,128]{1,0:T(8,128)(2,1)S(1)}, u32[]{:S(2)}, u32[]{:S(2)}) collective-permute-start(bf16[2480,128]{1,0:T(8,128)(2,1)S(1)} %spectra.1.b2), channel_id=1, source_target_pairs={{0,496},{8,24},{16,0},{24,40},{32,16},{40,56},{48,32},{56,72},{64,... | collective-permute-start | bytes 1904648 | tf_op jit(solution)/shard_map/ppermute | solution.py:386
  10.1 10.8 %collective-permute-start.3 = (bf16[2480,128]{1,0:T(8,128)(2,1)S(1)}, bf16[2480,128]{1,0:T(8,128)(2,1)S(1)}, u32[]{:S(2)}, u32[]{:S(2)}) collective-permute-start(bf16[2480,128]{1,0:T(8,128)(2,1)S(1)} %spectra.1.b2), channel_id=1, source_target_pairs={{0,16},{8,504},{16,32},{24,8},{32,48},{40,24},{48,64},{56,40},{64,... | collective-permute-start | bytes 1904648 | tf_op jit(solution)/shard_map/ppermute | solution.py:386
  20.9 2.9 %collective-permute-start.1 = (bf16[2480,128]{1,0:T(8,128)(2,1)S(1)}, bf16[2480,128]{1,0:T(8,128)(2,1)S(1)}, u32[]{:S(2)}, u32[]{:S(2)}) collective-permute-start(bf16[2480,128]{1,0:T(8,128)(2,1)S(1)} %spectra.1.b2), channel_id=1, source_target_pairs={{0,8},{8,0},{16,24},{24,16},{32,40},{40,32},{48,56},{56,48},{64,72... | collective-permute-start | bytes 1904648 | tf_op jit(solution)/shard_map/ppermute | solution.py:381
  23.8 2.9 %collective-permute-done.b0 = bf16[2480,128]{1,0:T(8,128)(2,1)S(1)} collective-permute-done((bf16[2480,128]{1,0:T(8,128)(2,1)S(1)}, bf16[2480,128]{1,0:T(8,128)(2,1)S(1)}, u32[]{:S(2)}, u32[]{:S(2)}) %collective-permute-start) | collective-permute-done | bytes 634912 | tf_op jit(solution)/shard_map/ppermute | solution.py:386
  26.7 9.0 %collective-permute-start.2 = (bf16[2480,128]{1,0:T(8,128)(2,1)S(1)}, bf16[2480,128]{1,0:T(8,128)(2,1)S(1)}, u32[]{:S(2)}, u32[]{:S(2)}) collective-permute-start(bf16[2480,128]{1,0:T(8,128)(2,1)S(1)} %collective-permute-done.b0), channel_id=1, source_target_pairs={{0,8},{8,0},{16,24},{24,16},{32,40},{40,32},{48,56},{56,48},{64,72... | collective-permute-start | bytes 1904648 | tf_op jit(solution)/shard_map/ppermute | solution.py:381
  35.7 0.0 collective-permute-done.3.b4
  35.7 0.0 collective-permute-done.1.b1
  35.8 1.7 %collective-permute-done.2.b3 = bf16[2480,128]{1,0:T(8,128)(2,1)S(1)} collective-permute-done((bf16[2480,128]{1,0:T(8,128)(2,1)S(1)}, bf16[2480,128]{1,0:T(8,128)(2,1)S(1)}, u32[]{:S(2)}, u32[]{:S(2)}) %collective-permute-start.2) | collective-permute-done | bytes 634912 | tf_op jit(solution)/shard_map/ppermute | solution.py:381
  37.4 0.0 copy-done
  37.4 1.1 %pair_rows.1 = bf16[8,192,128]{2,1,0:T(8,128)(2,1)S(1)} custom-call(bf16[2480,128]{1,0:T(8,128)(2,1)S(1)} %collective-permute-done.b0, bf16[2480,128]{1,0:T(8,128)(2,1)S(1)} %collective-permute-done.1.b1, bf16[2480,128]{1,0:T(8,128)(2,1)S(1)} %spectra.1.b2, bf16[2480,128]{1,0:T(8,128)(2,1)S(1)} %collective-permute-done.2.b3, ...), custom_call_target="tpu_custom_call" | custom-call | tf_op jit(solution)/shard_map/pair_rows/pallas_call | solution.py:338
  38.5 20.5 %all_to_all.5 = bf16[8,192,128]{2,1,0:T(8,128)(2,1)S(1)} all-to-all(bf16[8,192,128]{2,1,0:T(8,128)(2,1)S(1)} %pair_rows.1), channel_id=1, replica_groups=mesh['fibre'=64,'tm'=8] {'tm'}, dimensions={0} | all-to-all | bytes 786432 | tf_op jit(solution)/shard_map/all_to_all | solution.py:403
  59.0 0.1 convert_reduce_fusion
  59.1 7.4 %collective-permute-start.4 = (bf16[192,128]{1,0:T(8,128)(2,1)S(1)}, bf16[192,128]{1,0:T(8,128)(2,1)S(1)}, u32[]{:S(2)}, u32[]{:S(2)}) collective-permute-start(bf16[192,128]{1,0:T(8,128)(2,1)S(1)} %multiply_convert_fusion), channel_id=1, source_target_pairs={{0,496},{8,504},{16,0},{24,8},{32,16},{40,24},{48,32},{56,40},{64,... | collective-permute-start | bytes 147464 | tf_op jit(solution)/shard_map/ppermute | solution.py:376
  66.5 1.2 %collective-permute-done.4.row_ref = bf16[192,128]{1,0:T(8,128)(2,1)S(1)} collective-permute-done((bf16[192,128]{1,0:T(8,128)(2,1)S(1)}, bf16[192,128]{1,0:T(8,128)(2,1)S(1)}, u32[]{:S(2)}, u32[]{:S(2)}) %collective-permute-start.4) | collective-permute-done | bytes 49184 | tf_op jit(solution)/shard_map/ppermute | solution.py:376
  67.7 0.0 copy-done.1
  67.7 1.0 %lag_rows.1 = f32[401,1,128]{2,1,0:T(1,128)} custom-call(bf16[192,128]{1,0:T(8,128)(2,1)S(1)} %collective-permute-done.4.row_ref, bf16[401,384]{1,0:T(8,128)(2,1)S(1)} %copy-done.1), custom_call_target="tpu_custom_call" | custom-call | tf_op jit(solution)/shard_map/lag_rows/pallas_call | solution.py:364
  (1 shorter events, 0.0 us)
Async XLA Ops:
  0.7 36.8 %copy-start = (f32[192,1216]{1,0:T(8,128)S(1)}, f32[192,1216]{1,0:T(8,128)}, u32[]{:S(2)}) copy-start(f32[192,1216]{1,0:T(8,128)} %constant.14.clone.inner_ref) | copy-start | bytes 2801668
  5.1 62.6 %copy-start.1 = (bf16[401,384]{1,0:T(8,128)(2,1)S(1)}, bf16[401,384]{1,0:T(8,128)(2,1)}, u32[]{:S(2)}) copy-start(bf16[401,384]{1,0:T(8,128)(2,1)} %constant.15.clone.outer_ref) | copy-start | bytes 923908
  5.1 21.6 %collective-permute-start = (bf16[2480,128]{1,0:T(8,128)(2,1)S(1)}, bf16[2480,128]{1,0:T(8,128)(2,1)S(1)}, u32[]{:S(2)}, u32[]{:S(2)}) collective-permute-start(bf16[2480,128]{1,0:T(8,128)(2,1)S(1)} %spectra.1.b2), channel_id=1, source_target_pairs={{0,496},{8,24},{16,0},{24,40},{32,16},{40,56},{48,32},{56,72},{64,... | collective-permute-start | bytes 1904648 | tf_op jit(solution)/shard_map/ppermute | solution.py:386
  10.1 25.6 %collective-permute-start.3 = (bf16[2480,128]{1,0:T(8,128)(2,1)S(1)}, bf16[2480,128]{1,0:T(8,128)(2,1)S(1)}, u32[]{:S(2)}, u32[]{:S(2)}) collective-permute-start(bf16[2480,128]{1,0:T(8,128)(2,1)S(1)} %spectra.1.b2), channel_id=1, source_target_pairs={{0,16},{8,504},{16,32},{24,8},{32,48},{40,24},{48,64},{56,40},{64,... | collective-permute-start | bytes 1904648 | tf_op jit(solution)/shard_map/ppermute | solution.py:386
  20.9 14.9 %collective-permute-start.1 = (bf16[2480,128]{1,0:T(8,128)(2,1)S(1)}, bf16[2480,128]{1,0:T(8,128)(2,1)S(1)}, u32[]{:S(2)}, u32[]{:S(2)}) collective-permute-start(bf16[2480,128]{1,0:T(8,128)(2,1)S(1)} %spectra.1.b2), channel_id=1, source_target_pairs={{0,8},{8,0},{16,24},{24,16},{32,40},{40,32},{48,56},{56,48},{64,72... | collective-permute-start | bytes 1904648 | tf_op jit(solution)/shard_map/ppermute | solution.py:381
  26.7 10.7 %collective-permute-start.2 = (bf16[2480,128]{1,0:T(8,128)(2,1)S(1)}, bf16[2480,128]{1,0:T(8,128)(2,1)S(1)}, u32[]{:S(2)}, u32[]{:S(2)}) collective-permute-start(bf16[2480,128]{1,0:T(8,128)(2,1)S(1)} %collective-permute-done.b0), channel_id=1, source_target_pairs={{0,8},{8,0},{16,24},{24,16},{32,40},{40,32},{48,56},{56,48},{64,72... | collective-permute-start | bytes 1904648 | tf_op jit(solution)/shard_map/ppermute | solution.py:381
  59.1 8.6 %collective-permute-start.4 = (bf16[192,128]{1,0:T(8,128)(2,1)S(1)}, bf16[192,128]{1,0:T(8,128)(2,1)S(1)}, u32[]{:S(2)}, u32[]{:S(2)}) collective-permute-start(bf16[192,128]{1,0:T(8,128)(2,1)S(1)} %multiply_convert_fusion), channel_id=1, source_target_pairs={{0,496},{8,504},{16,0},{24,8},{32,16},{40,24},{48,32},{56,40},{64,... | collective-permute-start | bytes 147464 | tf_op jit(solution)/shard_map/ppermute | solution.py:376

commit v7 on v6

--- a/solution.py
+++ b/solution.py
@@ -37,7 +37,7 @@
 RANK = 2 * HALF
 STEP = 40
 STEPS = PN // STEP
-UNROLL = 19
+UNROLL = 38
 FRONT_VMEM = 28 * 2**20
 BF = jnp.bfloat16
 F32 = jnp.float32
@@ -66,10 +66,13 @@
     return COS[np.mod(index - TS // 4, TS)]
 
 
-def split(table):
-    high = np.asarray(table, np.float32).astype(BF)
-    low = (table - high.astype(np.float64)).astype(np.float32).astype(BF)
-    return high, low
+def split(table, parts=2):
+    rest = np.asarray(table, np.float64)
+    found = []
+    for _ in range(parts):
+        found.append(rest.astype(np.float32).astype(BF))
+        rest = rest - found[-1].astype(np.float64)
+    return found
 
 
 def bin_slots():
@@ -91,11 +94,10 @@
     weights = np.zeros((2 * KPAD, QPAD))
     weights[:KN, :QN] = cosine(PN * residue * q)
     weights[KPAD : KPAD + KN, :QN] = -sine(PN * residue * q)
-    high, low = split(weights)
+    high, mid, low = split(weights, 3)
     zero = np.zeros_like(low)
-    return np.concatenate(
-        [np.concatenate([high, high], 1), np.concatenate([low, zero], 1)], 0
-    )
+    rows = ([high, high, high], [mid, mid, zero], [low, zero, zero])
+    return np.concatenate([np.concatenate(row, 1) for row in rows], 0)
 
 
 def second_matrix():
@@ -110,8 +112,7 @@
     weights[:, :SLOT, PN:] = live * sign * sin
     weights[:, SLOT:, :PN] = -live * sin
     weights[:, SLOT:, PN:] = live * sign * cos
-    high, low = split(weights)
-    return np.concatenate([high, low], 1)
+    return np.concatenate(split(weights, 3), 1)
 
 
 def basis(table):
@@ -153,10 +154,12 @@
     return outer, inner.reshape(RANK, BINS).astype(np.float32)
 
 
-def halves(value):
+def thirds(value):
     high = value.astype(BF)
-    low = (value - high.astype(F32)).astype(BF)
-    return high, low
+    rest = value - high.astype(F32)
+    mid = rest.astype(BF)
+    low = (rest - mid.astype(F32)).astype(BF)
+    return high, mid, low
 
 
 def dot(left, right):
@@ -188,9 +191,9 @@
         for s in range(STEP):
             pad[0:QN, s * 128 : (s + 1) * 128] = flat[pl.ds(s, QN, stride=STEP), :]
         for pair in range(STEP // 2):
-            high, low = halves(pad[:, pair * 256 : (pair + 1) * 256])
-            both = dot(first[...], jnp.concatenate([high, low], 0))
-            section = both[: 2 * KPAD] + both[2 * KPAD :]
+            parts = thirds(pad[:, pair * 256 : (pair + 1) * 256])
+            full = dot(first[...], jnp.concatenate(parts, 0))
+            section = full[: 2 * KPAD] + (full[2 * KPAD : 4 * KPAD] + full[4 * KPAD :])
             for side in range(2):
                 p = g * STEP + pair * 2 + side
                 part = section[:, side * 128 : (side + 1) * 128]
@@ -203,9 +206,12 @@
     second_copy.wait()
 
     def residue(k, power):
-        high, low = halves(ts[pl.ds(pl.multiple_of(k * WIDE, 8), 2 * PN), :])
-        product = dot(second[k], jnp.concatenate([high, low], 1))
-        value = product[:GROUP, :128] + (product[:GROUP, 128:] + product[GROUP:, :128])
+        high, mid, low = thirds(ts[pl.ds(pl.multiple_of(k * WIDE, 8), 2 * PN), :])
+        table = second[k]
+        wide = dot(table, jnp.concatenate([high, mid], 1))
+        small = wide[:GROUP, 128:] + wide[GROUP : 2 * GROUP, :128]
+        least = wide[GROUP : 2 * GROUP, 128:] + wide[2 * GROUP :, :128] + dot(table[:GROUP], low)
+        value = wide[:GROUP, :128] + (small + least)
         at = pl.multiple_of(k * SLOT, SLOT)
         zs[pl.ds(at, SLOT), :] = value[:SLOT]
         zs[pl.ds(BINS + at, SLOT), :] = value[SLOT:]

time: 69 us -> 70.2 us (1.017)
  Pallas kernels: 6.5 us -> 7.65 us
    pallas_call x1, Pallas kernels: 4.43 us -> 5.58 us  [spectra(): pl.pallas_call(spectrum_kernel, in_specs=[hbm, pl.BlockSpec(memory_space=...]
where the time goes in v7:
time: 70.2 us; the launch traced here: 69.8 us
  starting transfers between devices  35.1 us (50%)
  blocking collectives  20.5 us (29%)
  Pallas kernels  7.65 us (11%)
  waiting for transfers between devices  5.75 us (8%)
  between operations  0.75 us (1%)
    all_to_all x1, blocking collectives, shards(): shared = lax.all_to_all(rows, 'tm', 0, 0)  20.5 us
    ppermute x2, starting transfers between devices, parted(): lax.ppermute(array, 'fibre', [(i, (i - by if i % 2 == 0 else i + by) % si...  15.7 us
    ppermute x2, starting transfers between devices, swapped(): return lax.ppermute(array, 'fibre', [(i, i ^ 1) for i in range(size)])  11.9 us
    ppermute x1, starting transfers between devices, turned(): lax.ppermute(array, 'fibre', [(i, (i + by) % size) for i in range(size)])  7.43 us
    pallas_call x1, Pallas kernels, spectra(): pl.pallas_call(spectrum_kernel, in_specs=[hbm, pl.BlockSpec(memory_space=...  5.58 us
    ppermute x2, waiting for transfers between devices, parted(): lax.ppermute(array, 'fibre', [(i, (i - by if i % 2 == 0 else i + by) % si...  2.94 us
    ppermute x2, waiting for transfers between devices, swapped(): return lax.ppermute(array, 'fibre', [(i, i ^ 1) for i in range(size)])  1.65 us
  transfers between devices with their start and end apart: 5, of which 3 were waited for; matrix products, arithmetic and copies ran while one was open for 0% of the time, Pallas kernels for 0%

profile of v7, /device:TPU:1, one launch (start us, length us, event | category | flops | bytes accessed | tf_op | source)
XLA Modules:
  0.0 69.8 jit_solution(15037572675977928182)
XLA Ops:
  0.7 0.0 copy-start
  0.7 5.6 %spectra.1.b2 = bf16[2480,128]{1,0:T(8,128)(2,1)S(1)} custom-call(s32[2,4]{1,0:T(2,128)} %bitcast.8, s32[1]{0:T(128)S(6)} %copy.9.count_ref, f32[75,80,128]{2,1,0:T(8,128)} %bitcast.7, bf16[240,240]{1,0:T(8,128)(2,1)} %constant.12.clone.first_hbm, bf16[38,192,160]{2,1,0:T(8,128)(2,1)} %constant.13.clone.second_hbm), custom_call_target="tpu_custom_call" | custom-call | tf_op jit(solution)/shard_map/spectra/pallas_call | solution.py:261
  6.3 0.0 copy-start.1
  6.3 5.0 %collective-permute-start = (bf16[2480,128]{1,0:T(8,128)(2,1)S(1)}, bf16[2480,128]{1,0:T(8,128)(2,1)S(1)}, u32[]{:S(2)}, u32[]{:S(2)}) collective-permute-start(bf16[2480,128]{1,0:T(8,128)(2,1)S(1)} %spectra.1.b2), channel_id=1, source_target_pairs={{0,496},{8,24},{16,0},{24,40},{32,16},{40,56},{48,32},{56,72},{64,... | collective-permute-start | bytes 1904648 | tf_op jit(solution)/shard_map/ppermute | solution.py:392
  11.2 10.8 %collective-permute-start.3 = (bf16[2480,128]{1,0:T(8,128)(2,1)S(1)}, bf16[2480,128]{1,0:T(8,128)(2,1)S(1)}, u32[]{:S(2)}, u32[]{:S(2)}) collective-permute-start(bf16[2480,128]{1,0:T(8,128)(2,1)S(1)} %spectra.1.b2), channel_id=1, source_target_pairs={{0,16},{8,504},{16,32},{24,8},{32,48},{40,24},{48,64},{56,40},{64,... | collective-permute-start | bytes 1904648 | tf_op jit(solution)/shard_map/ppermute | solution.py:392
  22.0 2.9 %collective-permute-start.1 = (bf16[2480,128]{1,0:T(8,128)(2,1)S(1)}, bf16[2480,128]{1,0:T(8,128)(2,1)S(1)}, u32[]{:S(2)}, u32[]{:S(2)}) collective-permute-start(bf16[2480,128]{1,0:T(8,128)(2,1)S(1)} %spectra.1.b2), channel_id=1, source_target_pairs={{0,8},{8,0},{16,24},{24,16},{32,40},{40,32},{48,56},{56,48},{64,72... | collective-permute-start | bytes 1904648 | tf_op jit(solution)/shard_map/ppermute | solution.py:387
  24.9 2.9 %collective-permute-done.b0 = bf16[2480,128]{1,0:T(8,128)(2,1)S(1)} collective-permute-done((bf16[2480,128]{1,0:T(8,128)(2,1)S(1)}, bf16[2480,128]{1,0:T(8,128)(2,1)S(1)}, u32[]{:S(2)}, u32[]{:S(2)}) %collective-permute-start) | collective-permute-done | bytes 634912 | tf_op jit(solution)/shard_map/ppermute | solution.py:392
  27.8 9.0 %collective-permute-start.2 = (bf16[2480,128]{1,0:T(8,128)(2,1)S(1)}, bf16[2480,128]{1,0:T(8,128)(2,1)S(1)}, u32[]{:S(2)}, u32[]{:S(2)}) collective-permute-start(bf16[2480,128]{1,0:T(8,128)(2,1)S(1)} %collective-permute-done.b0), channel_id=1, source_target_pairs={{0,8},{8,0},{16,24},{24,16},{32,40},{40,32},{48,56},{56,48},{64,72... | collective-permute-start | bytes 1904648 | tf_op jit(solution)/shard_map/ppermute | solution.py:387
  36.9 0.0 collective-permute-done.3.b4
  36.9 0.0 collective-permute-done.1.b1
  36.9 1.7 %collective-permute-done.2.b3 = bf16[2480,128]{1,0:T(8,128)(2,1)S(1)} collective-permute-done((bf16[2480,128]{1,0:T(8,128)(2,1)S(1)}, bf16[2480,128]{1,0:T(8,128)(2,1)S(1)}, u32[]{:S(2)}, u32[]{:S(2)}) %collective-permute-start.2) | collective-permute-done | bytes 634912 | tf_op jit(solution)/shard_map/ppermute | solution.py:387
  38.5 0.0 copy-done
  38.5 1.1 %pair_rows.1 = bf16[8,192,128]{2,1,0:T(8,128)(2,1)S(1)} custom-call(bf16[2480,128]{1,0:T(8,128)(2,1)S(1)} %collective-permute-done.b0, bf16[2480,128]{1,0:T(8,128)(2,1)S(1)} %collective-permute-done.1.b1, bf16[2480,128]{1,0:T(8,128)(2,1)S(1)} %spectra.1.b2, bf16[2480,128]{1,0:T(8,128)(2,1)S(1)} %collective-permute-done.2.b3, ...), custom_call_target="tpu_custom_call" | custom-call | tf_op jit(solution)/shard_map/pair_rows/pallas_call | solution.py:344
  39.6 20.5 %all_to_all.5 = bf16[8,192,128]{2,1,0:T(8,128)(2,1)S(1)} all-to-all(bf16[8,192,128]{2,1,0:T(8,128)(2,1)S(1)} %pair_rows.1), channel_id=1, replica_groups=mesh['fibre'=64,'tm'=8] {'tm'}, dimensions={0} | all-to-all | bytes 786432 | tf_op jit(solution)/shard_map/all_to_all | solution.py:409
  60.1 0.1 convert_reduce_fusion
  60.2 7.4 %collective-permute-start.4 = (bf16[192,128]{1,0:T(8,128)(2,1)S(1)}, bf16[192,128]{1,0:T(8,128)(2,1)S(1)}, u32[]{:S(2)}, u32[]{:S(2)}) collective-permute-start(bf16[192,128]{1,0:T(8,128)(2,1)S(1)} %multiply_convert_fusion), channel_id=1, source_target_pairs={{0,496},{8,504},{16,0},{24,8},{32,16},{40,24},{48,32},{56,40},{64,... | collective-permute-start | bytes 147464 | tf_op jit(solution)/shard_map/ppermute | solution.py:382
  67.6 1.2 %collective-permute-done.4.row_ref = bf16[192,128]{1,0:T(8,128)(2,1)S(1)} collective-permute-done((bf16[192,128]{1,0:T(8,128)(2,1)S(1)}, bf16[192,128]{1,0:T(8,128)(2,1)S(1)}, u32[]{:S(2)}, u32[]{:S(2)}) %collective-permute-start.4) | collective-permute-done | bytes 49184 | tf_op jit(solution)/shard_map/ppermute | solution.py:382
  68.8 0.0 copy-done.1
  68.8 1.0 %lag_rows.1 = f32[401,1,128]{2,1,0:T(1,128)} custom-call(bf16[192,128]{1,0:T(8,128)(2,1)S(1)} %collective-permute-done.4.row_ref, bf16[401,384]{1,0:T(8,128)(2,1)S(1)} %copy-done.1), custom_call_target="tpu_custom_call" | custom-call | tf_op jit(solution)/shard_map/lag_rows/pallas_call | solution.py:370
  (1 shorter events, 0.0 us)
Async XLA Ops:
  0.7 37.9 %copy-start = (f32[192,1216]{1,0:T(8,128)S(1)}, f32[192,1216]{1,0:T(8,128)}, u32[]{:S(2)}) copy-start(f32[192,1216]{1,0:T(8,128)} %constant.14.clone.inner_ref) | copy-start | bytes 2801668
  6.3 62.5 %copy-start.1 = (bf16[401,384]{1,0:T(8,128)(2,1)S(1)}, bf16[401,384]{1,0:T(8,128)(2,1)}, u32[]{:S(2)}) copy-start(bf16[401,384]{1,0:T(8,128)(2,1)} %constant.15.clone.outer_ref) | copy-start | bytes 923908
  6.3 21.6 %collective-permute-start = (bf16[2480,128]{1,0:T(8,128)(2,1)S(1)}, bf16[2480,128]{1,0:T(8,128)(2,1)S(1)}, u32[]{:S(2)}, u32[]{:S(2)}) collective-permute-start(bf16[2480,128]{1,0:T(8,128)(2,1)S(1)} %spectra.1.b2), channel_id=1, source_target_pairs={{0,496},{8,24},{16,0},{24,40},{32,16},{40,56},{48,32},{56,72},{64,... | collective-permute-start | bytes 1904648 | tf_op jit(solution)/shard_map/ppermute | solution.py:392
  11.2 25.6 %collective-permute-start.3 = (bf16[2480,128]{1,0:T(8,128)(2,1)S(1)}, bf16[2480,128]{1,0:T(8,128)(2,1)S(1)}, u32[]{:S(2)}, u32[]{:S(2)}) collective-permute-start(bf16[2480,128]{1,0:T(8,128)(2,1)S(1)} %spectra.1.b2), channel_id=1, source_target_pairs={{0,16},{8,504},{16,32},{24,8},{32,48},{40,24},{48,64},{56,40},{64,... | collective-permute-start | bytes 1904648 | tf_op jit(solution)/shard_map/ppermute | solution.py:392
  22.0 14.9 %collective-permute-start.1 = (bf16[2480,128]{1,0:T(8,128)(2,1)S(1)}, bf16[2480,128]{1,0:T(8,128)(2,1)S(1)}, u32[]{:S(2)}, u32[]{:S(2)}) collective-permute-start(bf16[2480,128]{1,0:T(8,128)(2,1)S(1)} %spectra.1.b2), channel_id=1, source_target_pairs={{0,8},{8,0},{16,24},{24,16},{32,40},{40,32},{48,56},{56,48},{64,72... | collective-permute-start | bytes 1904648 | tf_op jit(solution)/shard_map/ppermute | solution.py:387
  27.8 10.7 %collective-permute-start.2 = (bf16[2480,128]{1,0:T(8,128)(2,1)S(1)}, bf16[2480,128]{1,0:T(8,128)(2,1)S(1)}, u32[]{:S(2)}, u32[]{:S(2)}) collective-permute-start(bf16[2480,128]{1,0:T(8,128)(2,1)S(1)} %collective-permute-done.b0), channel_id=1, source_target_pairs={{0,8},{8,0},{16,24},{24,16},{32,40},{40,32},{48,56},{56,48},{64,72... | collective-permute-start | bytes 1904648 | tf_op jit(solution)/shard_map/ppermute | solution.py:387
  60.2 8.6 %collective-permute-start.4 = (bf16[192,128]{1,0:T(8,128)(2,1)S(1)}, bf16[192,128]{1,0:T(8,128)(2,1)S(1)}, u32[]{:S(2)}, u32[]{:S(2)}) collective-permute-start(bf16[192,128]{1,0:T(8,128)(2,1)S(1)} %multiply_convert_fusion), channel_id=1, source_target_pairs={{0,496},{8,504},{16,0},{24,8},{32,16},{40,24},{48,32},{56,40},{64,... | collective-permute-start | bytes 147464 | tf_op jit(solution)/shard_map/ppermute | solution.py:382

commit v8 on v7

--- a/solution.py
+++ b/solution.py
@@ -172,7 +172,7 @@
 ):
     def load(g):
         return pltpu.make_async_copy(
-            x_hbm.at[:, pl.ds(g * STEP, STEP), :], xs.at[g], sems.at[g]
+            x_hbm.at[:, pl.ds(g * STEP, STEP), :], xs.at[g, pl.ds(0, QN)], sems.at[g]
         )
 
     first_copy = pltpu.make_async_copy(first_hbm, first, sems.at[STEPS])
@@ -187,7 +187,7 @@
 
     def sections(g, carry):
         load(g).wait()
-        flat = xs.at[g].reshape(QN * STEP, 128)
+        flat = xs.at[g].reshape((QN + 1) * STEP, 128)
         for s in range(STEP):
             pad[0:QN, s * 128 : (s + 1) * 128] = flat[pl.ds(s, QN, stride=STEP), :]
         for pair in range(STEP // 2):
@@ -265,11 +265,11 @@
         out_shape=jax.ShapeDtypeStruct((ROWS, 128), BF),
         scratch_shapes=[
             pltpu.SMEM(pair_blocks.shape, jnp.int32),
-            pltpu.VMEM((STEPS, QN, STEP, 128), F32),
+            pltpu.VMEM((STEPS, QN + 1, STEP, 128), F32),
             pltpu.VMEM(first.shape, BF),
             pltpu.VMEM(second.shape, BF),
             pltpu.VMEM((QPAD, STEP * 128), F32),
-            pltpu.VMEM((KPAD * WIDE, 128), F32),
+            pltpu.VMEM(((KPAD + 1) * WIDE, 128), F32),
             pltpu.VMEM((FN, 128), F32),
             pltpu.VMEM((TAIL, 128), F32),
             pltpu.SemaphoreType.DMA((STEPS + 3,)),

time: 70.2 us -> 70.2 us (level)
  blocking collectives: 20.5 us -> 17.7 us
  starting transfers between devices: 35.1 us -> 37.8 us
    all_to_all x1, blocking collectives: 20.5 us -> 17.7 us  [shards(): shared = lax.all_to_all(rows, 'tm', 0, 0)]
    ppermute x1, starting transfers between devices: 7.43 us -> 10.2 us  [turned(): lax.ppermute(array, 'fibre', [(i, (i + by) % size) for i in range(size)])]
where the time goes in v8:
time: 70.2 us; the launch traced here: 69.8 us
  starting transfers between devices  37.8 us (54%)
  blocking collectives  17.7 us (25%)
  Pallas kernels  7.68 us (11%)
  waiting for transfers between devices  5.75 us (8%)
  between operations  0.75 us (1%)
    all_to_all x1, blocking collectives, shards(): shared = lax.all_to_all(rows, 'tm', 0, 0)  17.7 us
    ppermute x2, starting transfers between devices, parted(): lax.ppermute(array, 'fibre', [(i, (i - by if i % 2 == 0 else i + by) % si...  15.7 us
    ppermute x2, starting transfers between devices, swapped(): return lax.ppermute(array, 'fibre', [(i, i ^ 1) for i in range(size)])  11.9 us
    ppermute x1, starting transfers between devices, turned(): lax.ppermute(array, 'fibre', [(i, (i + by) % size) for i in range(size)])  10.2 us
    pallas_call x1, Pallas kernels, spectra(): pl.pallas_call(spectrum_kernel, in_specs=[hbm, pl.BlockSpec(memory_space=...  5.61 us
    ppermute x2, waiting for transfers between devices, parted(): lax.ppermute(array, 'fibre', [(i, (i - by if i % 2 == 0 else i + by) % si...  2.94 us
    ppermute x2, waiting for transfers between devices, swapped(): return lax.ppermute(array, 'fibre', [(i, i ^ 1) for i in range(size)])  1.65 us
  transfers between devices with their start and end apart: 5, of which 3 were waited for; matrix products, arithmetic and copies ran while one was open for 0% of the time, Pallas kernels for 0%

profile of v8, /device:TPU:1, one launch (start us, length us, event | category | flops | bytes accessed | tf_op | source)
XLA Modules:
  0.0 69.8 jit_solution(14476197397145628058)
XLA Ops:
  0.7 0.0 copy-start
  0.7 5.6 %spectra.1.b2 = bf16[2480,128]{1,0:T(8,128)(2,1)S(1)} custom-call(s32[2,4]{1,0:T(2,128)} %bitcast.8, s32[1]{0:T(128)S(6)} %copy.9.count_ref, f32[75,80,128]{2,1,0:T(8,128)} %bitcast.7, bf16[240,240]{1,0:T(8,128)(2,1)} %constant.12.clone.first_hbm, bf16[38,192,160]{2,1,0:T(8,128)(2,1)} %constant.13.clone.second_hbm), custom_call_target="tpu_custom_call" | custom-call | tf_op jit(solution)/shard_map/spectra/pallas_call | solution.py:261
  6.3 0.0 copy-start.1
  6.3 5.0 %collective-permute-start = (bf16[2480,128]{1,0:T(8,128)(2,1)S(1)}, bf16[2480,128]{1,0:T(8,128)(2,1)S(1)}, u32[]{:S(2)}, u32[]{:S(2)}) collective-permute-start(bf16[2480,128]{1,0:T(8,128)(2,1)S(1)} %spectra.1.b2), channel_id=1, source_target_pairs={{0,496},{8,24},{16,0},{24,40},{32,16},{40,56},{48,32},{56,72},{64,... | collective-permute-start | bytes 1904648 | tf_op jit(solution)/shard_map/ppermute | solution.py:392
  11.3 10.8 %collective-permute-start.3 = (bf16[2480,128]{1,0:T(8,128)(2,1)S(1)}, bf16[2480,128]{1,0:T(8,128)(2,1)S(1)}, u32[]{:S(2)}, u32[]{:S(2)}) collective-permute-start(bf16[2480,128]{1,0:T(8,128)(2,1)S(1)} %spectra.1.b2), channel_id=1, source_target_pairs={{0,16},{8,504},{16,32},{24,8},{32,48},{40,24},{48,64},{56,40},{64,... | collective-permute-start | bytes 1904648 | tf_op jit(solution)/shard_map/ppermute | solution.py:392
  22.1 2.9 %collective-permute-start.1 = (bf16[2480,128]{1,0:T(8,128)(2,1)S(1)}, bf16[2480,128]{1,0:T(8,128)(2,1)S(1)}, u32[]{:S(2)}, u32[]{:S(2)}) collective-permute-start(bf16[2480,128]{1,0:T(8,128)(2,1)S(1)} %spectra.1.b2), channel_id=1, source_target_pairs={{0,8},{8,0},{16,24},{24,16},{32,40},{40,32},{48,56},{56,48},{64,72... | collective-permute-start | bytes 1904648 | tf_op jit(solution)/shard_map/ppermute | solution.py:387
  24.9 2.9 %collective-permute-done.b0 = bf16[2480,128]{1,0:T(8,128)(2,1)S(1)} collective-permute-done((bf16[2480,128]{1,0:T(8,128)(2,1)S(1)}, bf16[2480,128]{1,0:T(8,128)(2,1)S(1)}, u32[]{:S(2)}, u32[]{:S(2)}) %collective-permute-start) | collective-permute-done | bytes 634912 | tf_op jit(solution)/shard_map/ppermute | solution.py:392
  27.9 9.0 %collective-permute-start.2 = (bf16[2480,128]{1,0:T(8,128)(2,1)S(1)}, bf16[2480,128]{1,0:T(8,128)(2,1)S(1)}, u32[]{:S(2)}, u32[]{:S(2)}) collective-permute-start(bf16[2480,128]{1,0:T(8,128)(2,1)S(1)} %collective-permute-done.b0), channel_id=1, source_target_pairs={{0,8},{8,0},{16,24},{24,16},{32,40},{40,32},{48,56},{56,48},{64,72... | collective-permute-start | bytes 1904648 | tf_op jit(solution)/shard_map/ppermute | solution.py:387
  36.9 0.0 collective-permute-done.3.b4
  36.9 0.0 collective-permute-done.1.b1
  36.9 1.7 %collective-permute-done.2.b3 = bf16[2480,128]{1,0:T(8,128)(2,1)S(1)} collective-permute-done((bf16[2480,128]{1,0:T(8,128)(2,1)S(1)}, bf16[2480,128]{1,0:T(8,128)(2,1)S(1)}, u32[]{:S(2)}, u32[]{:S(2)}) %collective-permute-start.2) | collective-permute-done | bytes 634912 | tf_op jit(solution)/shard_map/ppermute | solution.py:387
  38.6 0.0 copy-done
  38.6 1.1 %pair_rows.1 = bf16[8,192,128]{2,1,0:T(8,128)(2,1)S(1)} custom-call(bf16[2480,128]{1,0:T(8,128)(2,1)S(1)} %collective-permute-done.b0, bf16[2480,128]{1,0:T(8,128)(2,1)S(1)} %collective-permute-done.1.b1, bf16[2480,128]{1,0:T(8,128)(2,1)S(1)} %spectra.1.b2, bf16[2480,128]{1,0:T(8,128)(2,1)S(1)} %collective-permute-done.2.b3, ...), custom_call_target="tpu_custom_call" | custom-call | tf_op jit(solution)/shard_map/pair_rows/pallas_call | solution.py:344
  39.7 17.7 %all_to_all.5 = bf16[8,192,128]{2,1,0:T(8,128)(2,1)S(1)} all-to-all(bf16[8,192,128]{2,1,0:T(8,128)(2,1)S(1)} %pair_rows.1), channel_id=1, replica_groups=mesh['fibre'=64,'tm'=8] {'tm'}, dimensions={0} | all-to-all | bytes 786432 | tf_op jit(solution)/shard_map/all_to_all | solution.py:409
  57.4 0.1 convert_reduce_fusion
  57.5 10.2 %collective-permute-start.4 = (bf16[192,128]{1,0:T(8,128)(2,1)S(1)}, bf16[192,128]{1,0:T(8,128)(2,1)S(1)}, u32[]{:S(2)}, u32[]{:S(2)}) collective-permute-start(bf16[192,128]{1,0:T(8,128)(2,1)S(1)} %multiply_convert_fusion), channel_id=1, source_target_pairs={{0,496},{8,504},{16,0},{24,8},{32,16},{40,24},{48,32},{56,40},{64,... | collective-permute-start | bytes 147464 | tf_op jit(solution)/shard_map/ppermute | solution.py:382
  67.7 1.2 %collective-permute-done.4.row_ref = bf16[192,128]{1,0:T(8,128)(2,1)S(1)} collective-permute-done((bf16[192,128]{1,0:T(8,128)(2,1)S(1)}, bf16[192,128]{1,0:T(8,128)(2,1)S(1)}, u32[]{:S(2)}, u32[]{:S(2)}) %collective-permute-start.4) | collective-permute-done | bytes 49184 | tf_op jit(solution)/shard_map/ppermute | solution.py:382
  68.8 0.0 copy-done.1
  68.8 1.0 %lag_rows.1 = f32[401,1,128]{2,1,0:T(1,128)} custom-call(bf16[192,128]{1,0:T(8,128)(2,1)S(1)} %collective-permute-done.4.row_ref, bf16[401,384]{1,0:T(8,128)(2,1)S(1)} %copy-done.1), custom_call_target="tpu_custom_call" | custom-call | tf_op jit(solution)/shard_map/lag_rows/pallas_call | solution.py:370
  (1 shorter events, 0.0 us)
Async XLA Ops:
  0.7 37.9 %copy-start = (f32[192,1216]{1,0:T(8,128)S(1)}, f32[192,1216]{1,0:T(8,128)}, u32[]{:S(2)}) copy-start(f32[192,1216]{1,0:T(8,128)} %constant.14.clone.inner_ref) | copy-start | bytes 2801668
  6.3 62.5 %copy-start.1 = (bf16[401,384]{1,0:T(8,128)(2,1)S(1)}, bf16[401,384]{1,0:T(8,128)(2,1)}, u32[]{:S(2)}) copy-start(bf16[401,384]{1,0:T(8,128)(2,1)} %constant.15.clone.outer_ref) | copy-start | bytes 923908
  6.3 21.6 %collective-permute-start = (bf16[2480,128]{1,0:T(8,128)(2,1)S(1)}, bf16[2480,128]{1,0:T(8,128)(2,1)S(1)}, u32[]{:S(2)}, u32[]{:S(2)}) collective-permute-start(bf16[2480,128]{1,0:T(8,128)(2,1)S(1)} %spectra.1.b2), channel_id=1, source_target_pairs={{0,496},{8,24},{16,0},{24,40},{32,16},{40,56},{48,32},{56,72},{64,... | collective-permute-start | bytes 1904648 | tf_op jit(solution)/shard_map/ppermute | solution.py:392
  11.3 25.6 %collective-permute-start.3 = (bf16[2480,128]{1,0:T(8,128)(2,1)S(1)}, bf16[2480,128]{1,0:T(8,128)(2,1)S(1)}, u32[]{:S(2)}, u32[]{:S(2)}) collective-permute-start(bf16[2480,128]{1,0:T(8,128)(2,1)S(1)} %spectra.1.b2), channel_id=1, source_target_pairs={{0,16},{8,504},{16,32},{24,8},{32,48},{40,24},{48,64},{56,40},{64,... | collective-permute-start | bytes 1904648 | tf_op jit(solution)/shard_map/ppermute | solution.py:392
  22.1 14.8 %collective-permute-start.1 = (bf16[2480,128]{1,0:T(8,128)(2,1)S(1)}, bf16[2480,128]{1,0:T(8,128)(2,1)S(1)}, u32[]{:S(2)}, u32[]{:S(2)}) collective-permute-start(bf16[2480,128]{1,0:T(8,128)(2,1)S(1)} %spectra.1.b2), channel_id=1, source_target_pairs={{0,8},{8,0},{16,24},{24,16},{32,40},{40,32},{48,56},{56,48},{64,72... | collective-permute-start | bytes 1904648 | tf_op jit(solution)/shard_map/ppermute | solution.py:387
  27.9 10.7 %collective-permute-start.2 = (bf16[2480,128]{1,0:T(8,128)(2,1)S(1)}, bf16[2480,128]{1,0:T(8,128)(2,1)S(1)}, u32[]{:S(2)}, u32[]{:S(2)}) collective-permute-start(bf16[2480,128]{1,0:T(8,128)(2,1)S(1)} %collective-permute-done.b0), channel_id=1, source_target_pairs={{0,8},{8,0},{16,24},{24,16},{32,40},{40,32},{48,56},{56,48},{64,72... | collective-permute-start | bytes 1904648 | tf_op jit(solution)/shard_map/ppermute | solution.py:387
  57.5 11.4 %collective-permute-start.4 = (bf16[192,128]{1,0:T(8,128)(2,1)S(1)}, bf16[192,128]{1,0:T(8,128)(2,1)S(1)}, u32[]{:S(2)}, u32[]{:S(2)}) collective-permute-start(bf16[192,128]{1,0:T(8,128)(2,1)S(1)} %multiply_convert_fusion), channel_id=1, source_target_pairs={{0,496},{8,504},{16,0},{24,8},{32,16},{40,24},{48,32},{56,40},{64,... | collective-permute-start | bytes 147464 | tf_op jit(solution)/shard_map/ppermute | solution.py:382

commit v9 on v8

--- a/solution.py
+++ b/solution.py
@@ -389,9 +389,8 @@
 
 def parted(array, by):
     size = lax.axis_size("fibre")
-    return lax.ppermute(
-        array, "fibre", [(i, (i - by if i % 2 == 0 else i + by) % size) for i in range(size)]
-    )
+    steps = [(i, i - by if i % 2 == 0 else i + by) for i in range(size)]
+    return lax.ppermute(array, "fibre", [(i, to % size) for i, to in steps if to >= 0])
 
 
 def gathered(own):

time: 70.2 us -> 68.4 us (0.974)
  the two profiles are of different devices: /device:TPU:1 before, /device:TPU:6 now
where the time goes in v9:
time: 68.4 us; the launch traced here: 67.1 us
  starting transfers between devices  23.6 us (35%)
  blocking collectives  21.2 us (31%)
  waiting for transfers between devices  13.8 us (20%)
  Pallas kernels  7.68 us (11%)
  between operations  0.75 us (1%)
    all_to_all x1, blocking collectives, shards(): shared = lax.all_to_all(rows, 'tm', 0, 0)  21.2 us
    ppermute x2, starting transfers between devices, parted(): lax.ppermute(array, 'fibre', [(i, to % size) for i, to in steps if to >= 0])  13.3 us
    ppermute x2, waiting for transfers between devices, parted(): lax.ppermute(array, 'fibre', [(i, to % size) for i, to in steps if to >= 0])  10 us
    ppermute x1, starting transfers between devices, turned(): lax.ppermute(array, 'fibre', [(i, (i + by) % size) for i in range(size)])  6.5 us
    pallas_call x1, Pallas kernels, spectra(): pl.pallas_call(spectrum_kernel, in_specs=[hbm, pl.BlockSpec(memory_space=...  5.61 us
    ppermute x2, starting transfers between devices, swapped(): return lax.ppermute(array, 'fibre', [(i, i ^ 1) for i in range(size)])  3.83 us
    ppermute x2, waiting for transfers between devices, swapped(): return lax.ppermute(array, 'fibre', [(i, i ^ 1) for i in range(size)])  2.02 us
    ppermute x1, waiting for transfers between devices, turned(): lax.ppermute(array, 'fibre', [(i, (i + by) % size) for i in range(size)])  1.73 us
  transfers between devices with their start and end apart: 5, of which 3 were waited for; matrix products, arithmetic and copies ran while one was open for 0% of the time, Pallas kernels for 0%

profile of v9, /device:TPU:6, one launch (start us, length us, event | category | flops | bytes accessed | tf_op | source)
XLA Modules:
  0.0 67.1 jit_solution(17255647757016643472)
XLA Ops:
  0.7 0.0 copy-start
  0.7 5.6 %spectra.1.b2 = bf16[2480,128]{1,0:T(8,128)(2,1)S(1)} custom-call(s32[2,4]{1,0:T(2,128)} %bitcast.8, s32[1]{0:T(128)S(6)} %copy.9.count_ref, f32[75,80,128]{2,1,0:T(8,128)} %bitcast.7, bf16[240,240]{1,0:T(8,128)(2,1)} %constant.12.clone.first_hbm, bf16[38,192,160]{2,1,0:T(8,128)(2,1)} %constant.13.clone.second_hbm), custom_call_target="tpu_custom_call" | custom-call | tf_op jit(solution)/shard_map/spectra/pallas_call | solution.py:261
  6.3 0.0 copy-start.1
  6.3 11.3 %collective-permute-start = (bf16[2480,128]{1,0:T(8,128)(2,1)S(1)}, bf16[2480,128]{1,0:T(8,128)(2,1)S(1)}, u32[]{:S(2)}, u32[]{:S(2)}) collective-permute-start(bf16[2480,128]{1,0:T(8,128)(2,1)S(1)} %spectra.1.b2), channel_id=1, source_target_pairs={{8,24},{16,0},{24,40},{32,16},{40,56},{48,32},{56,72},{64,48},{72,... | collective-permute-start | bytes 1904648 | tf_op jit(solution)/shard_map/ppermute | solution.py:393
  17.6 1.9 %collective-permute-start.3 = (bf16[2480,128]{1,0:T(8,128)(2,1)S(1)}, bf16[2480,128]{1,0:T(8,128)(2,1)S(1)}, u32[]{:S(2)}, u32[]{:S(2)}) collective-permute-start(bf16[2480,128]{1,0:T(8,128)(2,1)S(1)} %spectra.1.b2), channel_id=1, source_target_pairs={{0,16},{16,32},{24,8},{32,48},{40,24},{48,64},{56,40},{64,80},{72,... | collective-permute-start | bytes 1904648 | tf_op jit(solution)/shard_map/ppermute | solution.py:393
  19.6 1.9 %collective-permute-start.1 = (bf16[2480,128]{1,0:T(8,128)(2,1)S(1)}, bf16[2480,128]{1,0:T(8,128)(2,1)S(1)}, u32[]{:S(2)}, u32[]{:S(2)}) collective-permute-start(bf16[2480,128]{1,0:T(8,128)(2,1)S(1)} %spectra.1.b2), channel_id=1, source_target_pairs={{0,8},{8,0},{16,24},{24,16},{32,40},{40,32},{48,56},{56,48},{64,72... | collective-permute-start | bytes 1904648 | tf_op jit(solution)/shard_map/ppermute | solution.py:387
  21.5 10.0 %collective-permute-done.b0 = bf16[2480,128]{1,0:T(8,128)(2,1)S(1)} collective-permute-done((bf16[2480,128]{1,0:T(8,128)(2,1)S(1)}, bf16[2480,128]{1,0:T(8,128)(2,1)S(1)}, u32[]{:S(2)}, u32[]{:S(2)}) %collective-permute-start) | collective-permute-done | bytes 634912 | tf_op jit(solution)/shard_map/ppermute | solution.py:393
  31.5 1.9 %collective-permute-start.2 = (bf16[2480,128]{1,0:T(8,128)(2,1)S(1)}, bf16[2480,128]{1,0:T(8,128)(2,1)S(1)}, u32[]{:S(2)}, u32[]{:S(2)}) collective-permute-start(bf16[2480,128]{1,0:T(8,128)(2,1)S(1)} %collective-permute-done.b0), channel_id=1, source_target_pairs={{0,8},{8,0},{16,24},{24,16},{32,40},{40,32},{48,56},{56,48},{64,72... | collective-permute-start | bytes 1904648 | tf_op jit(solution)/shard_map/ppermute | solution.py:387
  33.5 0.0 collective-permute-done.3.b4
  33.5 0.0 collective-permute-done.1.b1
  33.5 2.0 %collective-permute-done.2.b3 = bf16[2480,128]{1,0:T(8,128)(2,1)S(1)} collective-permute-done((bf16[2480,128]{1,0:T(8,128)(2,1)S(1)}, bf16[2480,128]{1,0:T(8,128)(2,1)S(1)}, u32[]{:S(2)}, u32[]{:S(2)}) %collective-permute-start.2) | collective-permute-done | bytes 634912 | tf_op jit(solution)/shard_map/ppermute | solution.py:387
  35.5 0.0 copy-done
  35.5 1.1 %pair_rows.1 = bf16[8,192,128]{2,1,0:T(8,128)(2,1)S(1)} custom-call(bf16[2480,128]{1,0:T(8,128)(2,1)S(1)} %collective-permute-done.b0, bf16[2480,128]{1,0:T(8,128)(2,1)S(1)} %collective-permute-done.1.b1, bf16[2480,128]{1,0:T(8,128)(2,1)S(1)} %spectra.1.b2, bf16[2480,128]{1,0:T(8,128)(2,1)S(1)} %collective-permute-done.2.b3, ...), custom_call_target="tpu_custom_call" | custom-call | tf_op jit(solution)/shard_map/pair_rows/pallas_call | solution.py:344
  36.6 21.2 %all_to_all.5 = bf16[8,192,128]{2,1,0:T(8,128)(2,1)S(1)} all-to-all(bf16[8,192,128]{2,1,0:T(8,128)(2,1)S(1)} %pair_rows.1), channel_id=1, replica_groups=mesh['fibre'=64,'tm'=8] {'tm'}, dimensions={0} | all-to-all | bytes 786432 | tf_op jit(solution)/shard_map/all_to_all | solution.py:408
  57.8 0.1 convert_reduce_fusion
  57.9 6.5 %collective-permute-start.4 = (bf16[192,128]{1,0:T(8,128)(2,1)S(1)}, bf16[192,128]{1,0:T(8,128)(2,1)S(1)}, u32[]{:S(2)}, u32[]{:S(2)}) collective-permute-start(bf16[192,128]{1,0:T(8,128)(2,1)S(1)} %multiply_convert_fusion), channel_id=1, source_target_pairs={{0,496},{8,504},{16,0},{24,8},{32,16},{40,24},{48,32},{56,40},{64,... | collective-permute-start | bytes 147464 | tf_op jit(solution)/shard_map/ppermute | solution.py:382
  64.4 1.7 %collective-permute-done.4.row_ref = bf16[192,128]{1,0:T(8,128)(2,1)S(1)} collective-permute-done((bf16[192,128]{1,0:T(8,128)(2,1)S(1)}, bf16[192,128]{1,0:T(8,128)(2,1)S(1)}, u32[]{:S(2)}, u32[]{:S(2)}) %collective-permute-start.4) | collective-permute-done | bytes 49184 | tf_op jit(solution)/shard_map/ppermute | solution.py:382
  66.1 0.0 copy-done.1
  66.1 1.0 %lag_rows.1 = f32[401,1,128]{2,1,0:T(1,128)} custom-call(bf16[192,128]{1,0:T(8,128)(2,1)S(1)} %collective-permute-done.4.row_ref, bf16[401,384]{1,0:T(8,128)(2,1)S(1)} %copy-done.1), custom_call_target="tpu_custom_call" | custom-call | tf_op jit(solution)/shard_map/lag_rows/pallas_call | solution.py:370
  (1 shorter events, 0.0 us)
Async XLA Ops:
  0.7 34.8 %copy-start = (f32[192,1216]{1,0:T(8,128)S(1)}, f32[192,1216]{1,0:T(8,128)}, u32[]{:S(2)}) copy-start(f32[192,1216]{1,0:T(8,128)} %constant.14.clone.inner_ref) | copy-start | bytes 2801668
  6.3 59.8 %copy-start.1 = (bf16[401,384]{1,0:T(8,128)(2,1)S(1)}, bf16[401,384]{1,0:T(8,128)(2,1)}, u32[]{:S(2)}) copy-start(bf16[401,384]{1,0:T(8,128)(2,1)} %constant.15.clone.outer_ref) | copy-start | bytes 923908
  6.3 25.2 %collective-permute-start = (bf16[2480,128]{1,0:T(8,128)(2,1)S(1)}, bf16[2480,128]{1,0:T(8,128)(2,1)S(1)}, u32[]{:S(2)}, u32[]{:S(2)}) collective-permute-start(bf16[2480,128]{1,0:T(8,128)(2,1)S(1)} %spectra.1.b2), channel_id=1, source_target_pairs={{8,24},{16,0},{24,40},{32,16},{40,56},{48,32},{56,72},{64,48},{72,... | collective-permute-start | bytes 1904648 | tf_op jit(solution)/shard_map/ppermute | solution.py:393
  17.6 15.8 %collective-permute-start.3 = (bf16[2480,128]{1,0:T(8,128)(2,1)S(1)}, bf16[2480,128]{1,0:T(8,128)(2,1)S(1)}, u32[]{:S(2)}, u32[]{:S(2)}) collective-permute-start(bf16[2480,128]{1,0:T(8,128)(2,1)S(1)} %spectra.1.b2), channel_id=1, source_target_pairs={{0,16},{16,32},{24,8},{32,48},{40,24},{48,64},{56,40},{64,80},{72,... | collective-permute-start | bytes 1904648 | tf_op jit(solution)/shard_map/ppermute | solution.py:393
  19.6 13.9 %collective-permute-start.1 = (bf16[2480,128]{1,0:T(8,128)(2,1)S(1)}, bf16[2480,128]{1,0:T(8,128)(2,1)S(1)}, u32[]{:S(2)}, u32[]{:S(2)}) collective-permute-start(bf16[2480,128]{1,0:T(8,128)(2,1)S(1)} %spectra.1.b2), channel_id=1, source_target_pairs={{0,8},{8,0},{16,24},{24,16},{32,40},{40,32},{48,56},{56,48},{64,72... | collective-permute-start | bytes 1904648 | tf_op jit(solution)/shard_map/ppermute | solution.py:387
  31.5 4.0 %collective-permute-start.2 = (bf16[2480,128]{1,0:T(8,128)(2,1)S(1)}, bf16[2480,128]{1,0:T(8,128)(2,1)S(1)}, u32[]{:S(2)}, u32[]{:S(2)}) collective-permute-start(bf16[2480,128]{1,0:T(8,128)(2,1)S(1)} %collective-permute-done.b0), channel_id=1, source_target_pairs={{0,8},{8,0},{16,24},{24,16},{32,40},{40,32},{48,56},{56,48},{64,72... | collective-permute-start | bytes 1904648 | tf_op jit(solution)/shard_map/ppermute | solution.py:387
  57.9 8.2 %collective-permute-start.4 = (bf16[192,128]{1,0:T(8,128)(2,1)S(1)}, bf16[192,128]{1,0:T(8,128)(2,1)S(1)}, u32[]{:S(2)}, u32[]{:S(2)}) collective-permute-start(bf16[192,128]{1,0:T(8,128)(2,1)S(1)} %multiply_convert_fusion), channel_id=1, source_target_pairs={{0,496},{8,504},{16,0},{24,8},{32,16},{40,24},{48,32},{56,40},{64,... | collective-permute-start | bytes 147464 | tf_op jit(solution)/shard_map/ppermute | solution.py:382
